TPU v7x, 256 devices: a whole 4x4x8 slice. The times are simulated.
256 devices in a mesh: grp: 8 (over z_lo, core), row: 32 (over y, z_hi, x).
Axes of the slice: x: 4, y: 4, z: 8 (z_hi: 2, z_lo: 4; z = z_hi * 4 + z_lo), core: 2. Of those that a mesh axis runs over, the one named last changes fastest.
Arguments:
- coefficients: float32 [2, 24576, 1024], P(None, 'row', 'grp'), may hold values from -6 to 6
- hamiltonian: bfloat16 [384, 12, 64, 128], P('row'), may hold values from -0.15625 to 0.15625
- neighbours: int32 [384, 12], P('row'), may hold values from 0 to 383, as said below
- positions: float32 [3, 384], replicated, may hold values from -4 to 4
- atom_site: int32 [384], replicated, may hold values from 0 to 16383
- rs_field: float32 [6, 256, 128, 128], P(None, ('grp', 'row')), may hold values from -6 to 6
- potential: float32 [3, 256, 128, 128], P(None, ('grp', 'row')), may hold values from -6 to 6
Outputs:
- coefficients_out: float32 [2, 24576, 1024], P(None, 'row', 'grp')
- field_out: float32 [6, 256, 128, 128], P(None, ('grp', 'row'))
- potential_out: float32 [3, 256, 128, 128], P(None, ('grp', 'row'))
Inputs may be any that keep to these rules, and one draw needn't show every extreme that they name: `neighbours`: each row's first block is the cluster itself, the second and third the clusters 6 after and 6 before it (a cluster beyond an end of the list is replaced by its mirror, the cluster as far on the other side); the others lie within 6 clusters of the row and may repeat. Every entry lies within 6 clusters of its row.
All inputs are finite; a program needn't handle non-finite values.
Results may differ from a plain program's by a relative error of at most 0.005.
Values may be sent and summed in bfloat16 or wider, within the bound.
A program may use at most 128 MiB of HBM per device.

v0:
```python
import math

import jax
import jax.numpy as jnp
from jax import lax
from jax.sharding import PartitionSpec as P

TERMS = 3


coupling = 0.7
elec_step = 1.5
wave_step = 0.5


def with_halo(block, sides, width):
    for axis, dim in sides:
        count = lax.axis_size(axis)
        forward = [(i, i + 1) for i in range(count - 1)]
        backward = [(target, source) for source, target in forward]
        low = lax.ppermute(
            lax.slice_in_dim(block, block.shape[dim] - width, None, axis=dim), axis, forward
        )
        high = lax.ppermute(lax.slice_in_dim(block, 0, width, axis=dim), axis, backward)
        block = jnp.concatenate([low, block, high], axis=dim)
    return block


def from_behind(value, axis, steps):
    count = lax.axis_size(axis)
    leading, last = (max(0, -steps), min(count, count - steps))
    return lax.ppermute(value, axis, [(source, source + steps) for source in range(leading, last)])


def as_sent(shard):

    def short(part):
        return part.astype(jnp.bfloat16) if part.dtype == jnp.float32 else part

    return jax.tree.map(short, shard)


def derivative(component, dim_index, forward):
    widths = [(0, 0), (0, 0), (0, 0)]
    widths[dim_index] = (0, 1) if forward else (1, 0)
    padded = jnp.pad(component, widths)
    extent = component.shape[dim_index]
    if forward:
        return lax.slice_in_dim(padded, 1, extent + 1, axis=dim_index) - component
    return component - lax.slice_in_dim(padded, 0, extent, axis=dim_index)


def plane_derivative(component, rim_plane, forward):
    if forward:
        return jnp.concatenate([component[1:], rim_plane], axis=0) - component
    return component - jnp.concatenate([rim_plane, component[:-1]], axis=0)


def curl_of(part, rim_planes, forward):
    comp_x, comp_y, comp_z = (part[0], part[1], part[2])
    first = derivative(comp_z, 1, forward) - derivative(comp_y, 2, forward)
    second = derivative(comp_x, 2, forward) - plane_derivative(comp_z, rim_planes[1], forward)
    third = plane_derivative(comp_y, rim_planes[0], forward) - derivative(comp_x, 1, forward)
    return jnp.stack([first, second, third])


def block_products(ph_real, ph_imag, part_real, part_imag, pattern):
    y_real = jnp.einsum(
        pattern, ph_real, part_real, preferred_element_type=jnp.float32
    ) - jnp.einsum(pattern, ph_imag, part_imag, preferred_element_type=jnp.float32)
    y_imag = jnp.einsum(
        pattern, ph_real, part_imag, preferred_element_type=jnp.float32
    ) + jnp.einsum(pattern, ph_imag, part_real, preferred_element_type=jnp.float32)
    return (y_real, y_imag)


def apply_blocks(taylor_term, ph_real, ph_imag, local_cols, reach, keep_blocks):
    atom_dev, nbr_count, orbitals = (ph_real.shape[0], ph_real.shape[1], ph_real.shape[2])
    bands = taylor_term.shape[2]
    own_rows = taylor_term.reshape(2, atom_dev, orbitals, bands)
    pattern = "anij,anjk->anik" if keep_blocks else "anij,anjk->aik"
    extended = with_halo(taylor_term, (("row", 1),), reach * orbitals)
    extended = extended.reshape(2, atom_dev + 2 * reach, orbitals, bands)
    picked = extended[:, local_cols]
    y_real, y_imag = block_products(ph_real, ph_imag, picked[0], picked[1], pattern)
    return (own_rows, y_real, y_imag)


def body(coefficients, hamiltonian, neighbours, positions, atom_site, rs_field, potential):
    atom_dev, orbitals = (hamiltonian.shape[0], hamiltonian.shape[2])
    reach = atom_dev // 2
    atoms_all = positions.shape[1]
    bands_dev = coefficients.shape[2]
    rows_dev = coefficients.shape[1]
    planes, grid_y, grid_z = (rs_field.shape[1], rs_field.shape[2], rs_field.shape[3])
    cells = planes * grid_y * grid_z
    total_planes = planes * lax.axis_size("grp") * lax.axis_size("row")
    current_scale = 1.0 / math.sqrt(2.0 * orbitals * bands_dev * lax.axis_size("grp"))
    first_atom = lax.axis_index("row") * atom_dev
    slab_start = lax.axis_index(("grp", "row")) * planes
    atom_ids = jnp.arange(atoms_all, dtype=jnp.int32)
    atom_plane = atom_ids * total_planes // atoms_all
    inside = (atom_plane >= slab_start) & (atom_plane < slab_start + planes)
    local_cell = (atom_plane - slab_start) * (grid_y * grid_z) + atom_site
    safe_cell = jnp.where(inside, local_cell, 0)
    drop_cell = jnp.where(inside, local_cell, cells)
    local_cols = neighbours - first_atom + reach
    own_pos = lax.dynamic_slice_in_dim(positions, first_atom, atom_dev, 1)
    bond_vectors = positions[:, neighbours] - own_pos[:, :, None]
    h_real = hamiltonian[..., :orbitals].astype(jnp.float32)
    h_imag = hamiltonian[..., orbitals:].astype(jnp.float32)
    wave_field = rs_field
    vector = potential
    flat_vector = vector.reshape(3, cells)
    looked = jnp.where(inside[None, :], flat_vector[:, safe_cell], 0.0)
    at_atoms = lax.psum(looked, ("grp", "row"))
    own_at = lax.dynamic_slice_in_dim(at_atoms, first_atom, atom_dev, 1)
    phase_angle = coupling * jnp.sum(
        0.5 * (own_at[:, :, None] + at_atoms[:, neighbours]) * bond_vectors, axis=0
    )
    cosine = jnp.cos(phase_angle)[:, :, None, None]
    sine_part = jnp.sin(phase_angle)[:, :, None, None]
    ph_real = (h_real * cosine - h_imag * sine_part).astype(jnp.bfloat16)
    ph_imag = (h_real * sine_part + h_imag * cosine).astype(jnp.bfloat16)
    taylor_term = coefficients.astype(jnp.bfloat16)
    running = coefficients
    for order_index in range(1, TERMS + 1):
        keep_blocks = order_index == 1
        own_rows, y_real, y_imag = apply_blocks(
            taylor_term, ph_real, ph_imag, local_cols, reach, keep_blocks
        )
        if keep_blocks:
            own_real = own_rows[0].astype(jnp.float32)
            own_imag = own_rows[1].astype(jnp.float32)
            block_share = jnp.einsum("aik,anik->an", own_real, y_imag) - jnp.einsum(
                "aik,anik->an", own_imag, y_real
            )
            own_current = current_scale * jnp.sum(bond_vectors * block_share[None], axis=2)
            sum_real = jnp.sum(y_real, axis=1)
            sum_imag = jnp.sum(y_imag, axis=1)
        else:
            sum_real = y_real
            sum_imag = y_imag
        factor = elec_step / order_index
        taylor_term = (
            jnp.stack([factor * sum_imag, -factor * sum_real])
            .reshape(2, rows_dev, bands_dev)
            .astype(jnp.bfloat16)
        )
        running = running + taylor_term.astype(jnp.float32)
    spread = lax.dynamic_update_slice_in_dim(
        jnp.zeros((3, atoms_all), jnp.float32), own_current, first_atom, 1
    )
    current = lax.psum(spread, ("grp", "row"))
    electric = wave_field[0:3]
    ahead_planes = from_behind(electric[1:3, :1].astype(jnp.bfloat16), ("grp", "row"), -1).astype(
        jnp.float32
    )
    magnetic = wave_field[3:6] - wave_step * curl_of(electric, ahead_planes, True)
    behind_planes = from_behind(as_sent(magnetic[1:3, -1:]), ("grp", "row"), 1)
    source = (
        jnp.zeros((3, cells), jnp.float32)
        .at[:, drop_cell]
        .add(current, mode="drop")
        .reshape(3, planes, grid_y, grid_z)
    )
    electric = electric + wave_step * (curl_of(magnetic, behind_planes, False) - source)
    vector = vector - wave_step * electric
    wave_field = jnp.concatenate([electric, magnetic], axis=0)
    return (running, wave_field, vector)


def solution(mesh):
    placed = (
        P(None, "row", "grp"),
        P("row", None, None, None),
        P("row", None),
        P(),
        P(),
        P(None, ("grp", "row"), None, None),
        P(None, ("grp", "row"), None, None),
    )
    return jax.shard_map(
        body,
        mesh=mesh,
        in_specs=placed,
        out_specs=(
            P(None, "row", "grp"),
            P(None, ("grp", "row"), None, None),
            P(None, ("grp", "row"), None, None),
        ),
        check_vma=False,
    )
```

profile of v0, /device:TPU:17, one launch (start us, length us, event | category | flops | bytes accessed | tf_op | source)
XLA Modules:
  0.0 304.0 jit_solution(16025253605299730857)
XLA Ops:
  0.7 1.2 convert_element_type.77
  2.7 3.1 %collective-permute-start = (bf16[2,384,128]{2,1,0:T(8,128)(2,1)}, bf16[2,384,128]{2,1,0:T(8,128)(2,1)}, u32[]{:S(2)}, u32[]{:S(2)}) collective-permute-start(bf16[2,384,128]{2,1,0:T(8,128)(2,1)} %get-tuple-element.18), channel_id=1, source_target_pairs={{0,1},{1,2},{2,3},{3,4},{4,5},{5,6},{6,7},{7,8},{8,9},{9,10},{10,1... | collective-permute-start | bytes 589832 | tf_op jit(solution)/shard_map/ppermute | solution.py:21
  5.8 9.7 %collective-permute-start.1 = (bf16[2,384,128]{2,1,0:T(8,128)(2,1)}, bf16[2,384,128]{2,1,0:T(8,128)(2,1)}, u32[]{:S(2)}, u32[]{:S(2)}) collective-permute-start(bf16[2,384,128]{2,1,0:T(8,128)(2,1)} %get-tuple-element.19), channel_id=1, source_target_pairs={{1,0},{2,1},{3,2},{4,3},{5,4},{6,5},{7,6},{8,7},{9,8},{10,9},{11,1... | collective-permute-start | bytes 589832 | tf_op jit(solution)/shard_map/ppermute | solution.py:24
  15.5 1.5 slice.372
  17.0 3.4 %collective-permute-start.6 = (bf16[2,1,128,128]{3,2,1,0:T(8,128)(2,1)}, bf16[2,1,128,128]{3,2,1,0:T(8,128)(2,1)}, u32[]{:S(2)}, u32[]{:S(2)}) collective-permute-start(bf16[2,1,128,128]{3,2,1,0:T(8,128)(2,1)} %slice.372), channel_id=1, source_target_pairs={{1,0},{2,1},{3,2},{4,3},{5,4},{6,5},{7,6},{8,7},{9,8},{10,9},{11,1... | collective-permute-start | bytes 196616 | tf_op jit(solution)/shard_map/ppermute | solution.py:32
  21.9 4.7 %copy.23 = f32[3,1,128,128]{0,3,2,1:T(8,128)} copy(f32[3,1,128,128]{3,2,1,0:T(8,128)S(1)} %copy-done.12) | data formatting | bytes 393216 | tf_op args[6]
  26.6 4.5 %gather_fusion = f32[384,3]{1,0:T(8,128)S(1)} fusion(f32[3,16384]{0,1:T(8,128)} %bitcast.243, s32[1024]{0:T(1024)S(1)} %pad_clamp_fusion.2), kind=kCustom, calls=%fused_computation | custom fusion | bytes 10752 | tf_op jit(solution)/shard_map/gather | solution.py:115
  31.3 76.3 %psum.14 = f32[3,384]{0,1:T(8,128)S(1)} all-reduce(f32[3,384]{0,1:T(8,128)S(1)} %select_bitcast_fusion), channel_id=1, replica_groups=mesh['grp'=8,'row'=32] {'grp','row'}, use_global_device_ids=true, to_apply=%region_0.1 | all-reduce | flops 1152 | bytes 9216 | tf_op jit(solution)/shard_map/psum | solution.py:116
  109.9 5.7 %fusion.7 = (bf16[12,12,64,64]{3,2,1,0:T(8,128)(2,1)S(1)}, bf16[12,12,64,64]{3,2,1,0:T(8,128)(2,1)}) fusion(f32[12,12]{1,0:T(8,128)S(1)} %get-tuple-element.28, f32[12,12]{1,0:T(8,128)S(1)} %get-tuple-element.27, bf16[12,12,64,128]{3,2,1,0:T(8,128)(2,1)} %param.8), kind=kLoop, calls=%fused_computation.18 | loop fusion | flops 5898240 | bytes 4719744 | tf_op jit(solution)/shard_map/convert_element_type | solution.py:124
  116.8 2.1 collective-permute-start.7
  119.6 10.8 %collective-permute-done.7 = bf16[2,1,128,128]{3,2,1,0:T(8,128)(2,1)S(1)} collective-permute-done((bf16[2,1,128,128]{3,2,1,0:T(8,128)(2,1)S(1)}, bf16[2,1,128,128]{3,2,1,0:T(8,128)(2,1)S(1)}, u32[]{:S(2)}, u32[]{:S(2)}) %collective-permute-start.7) | collective-permute-done | bytes 65568 | tf_op jit(solution)/shard_map/ppermute | solution.py:32
  131.1 1.1 pad_maximum_fusion
  132.2 7.6 %gather_fusion.3 = bf16[144,2,64,128]{3,2,1,0:T(8,128)(2,1)} fusion(bf16[2,24,64,128]{3,2,1,0:T(8,128)(2,1)S(1)} %bitcast.239, s32[1024]{0:T(1024)S(1)} %pad_clamp_fusion), kind=kCustom, calls=%fused_computation.3 | custom fusion | bytes 9437760 | tf_op jit(solution)/shard_map/gather | solution.py:84
  139.7 3.6 %copy.28 = bf16[144,2,64,128]{3,2,0,1:T(8,128)(2,1)S(1)} copy(bf16[144,2,64,128]{3,2,1,0:T(8,128)(2,1)} %gather_fusion.3) | data formatting | bytes 9437184 | tf_op jit(solution)/shard_map/gather | solution.py:84
  146.8 1.6 fusion
  148.4 1.6 fusion.2
  151.0 1.9 collective-permute-start.2
  153.0 10.3 %collective-permute-start.3 = (bf16[2,384,128]{2,1,0:T(8,128)(2,1)S(1)}, bf16[2,384,128]{2,1,0:T(8,128)(2,1)}, u32[]{:S(2)}, u32[]{:S(2)}) collective-permute-start(bf16[2,384,128]{2,1,0:T(8,128)(2,1)S(1)} %get-tuple-element.17), channel_id=1, source_target_pairs={{1,0},{2,1},{3,2},{4,3},{5,4},{6,5},{7,6},{8,7},{9,8},{10,9},{11,1... | collective-permute-start | bytes 589832 | tf_op jit(solution)/shard_map/ppermute | solution.py:24
  163.6 75.3 %psum.15 = f32[3,384]{0,1:T(8,128)S(1)} all-reduce(f32[3,384]{0,1:T(8,128)S(1)} %dynamic_update_slice.3), channel_id=1, replica_groups=mesh['grp'=8,'row'=32] {'grp','row'}, use_global_device_ids=true, to_apply=%region_5.6 | all-reduce | flops 1152 | bytes 9216 | tf_op jit(solution)/shard_map/psum | solution.py:154
  238.9 5.6 %scatter_custom_fusion = f32[3,16384]{0,1:T(8,128)} fusion(s32[384]{0:T(512)S(1)} %get-tuple-element.29, f32[]{:T(128)} %constant.10.clone.1, f32[3,384]{0,1:T(8,128)S(1)} %psum.15), kind=kCustom, calls=%fused_computation.19 | custom fusion | flops 1152 | bytes 393220 | tf_op jit(solution)/shard_map/scatter-add | solution.py:164
  244.5 5.9 %copy.32 = f32[3,1,128,128]{3,2,1,0:T(8,128)} copy(f32[3,1,128,128]{0,3,2,1:T(8,128)} %bitcast.242) | data formatting | bytes 393216 | tf_op jit(solution)/shard_map/reshape | solution.py:165
  251.0 1.1 pad_maximum_fusion.1
  252.1 7.6 %gather_fusion.4 = bf16[144,2,64,128]{3,2,1,0:T(8,128)(2,1)} fusion(bf16[2,24,64,128]{3,2,1,0:T(8,128)(2,1)S(1)} %bitcast.241, s32[1024]{0:T(1024)S(1)} %pad_clamp_fusion), kind=kCustom, calls=%fused_computation.4 | custom fusion | bytes 9437760 | tf_op jit(solution)/shard_map/gather | solution.py:84
  259.7 3.4 %copy.29 = bf16[144,2,64,128]{3,2,0,1:T(8,128)(2,1)S(1)} copy(bf16[144,2,64,128]{3,2,1,0:T(8,128)(2,1)} %gather_fusion.4) | data formatting | bytes 9437184 | tf_op jit(solution)/shard_map/gather | solution.py:84
  263.8 1.0 copy-done.1
  267.0 2.5 collective-permute-start.4
  269.5 10.0 %collective-permute-start.5 = (bf16[2,384,128]{2,1,0:T(8,128)(2,1)S(1)}, bf16[2,384,128]{2,1,0:T(8,128)(2,1)S(1)}, u32[]{:S(2)}, u32[]{:S(2)}) collective-permute-start(bf16[2,384,128]{2,1,0:T(8,128)(2,1)S(1)} %get-tuple-element.15), channel_id=1, source_target_pairs={{1,0},{2,1},{3,2},{4,3},{5,4},{6,5},{7,6},{8,7},{9,8},{10,9},{11,1... | collective-permute-start | bytes 589832 | tf_op jit(solution)/shard_map/ppermute | solution.py:24
  281.1 5.5 %collective-permute-done.4 = bf16[2,384,128]{2,1,0:T(8,128)(2,1)S(1)} collective-permute-done((bf16[2,384,128]{2,1,0:T(8,128)(2,1)S(1)}, bf16[2,384,128]{2,1,0:T(8,128)(2,1)S(1)}, u32[]{:S(2)}, u32[]{:S(2)}) %collective-permute-start.4) | collective-permute-done | bytes 196640 | tf_op jit(solution)/shard_map/ppermute | solution.py:21
  286.6 1.0 collective-permute-done.5
  287.7 7.6 %gather_fusion.5 = bf16[144,2,64,128]{3,2,1,0:T(8,128)(2,1)} fusion(bf16[2,24,64,128]{3,2,1,0:T(8,128)(2,1)S(1)} %bitcast.240, s32[1024]{0:T(1024)S(1)} %pad_clamp_fusion), kind=kCustom, calls=%fused_computation.5 | custom fusion | bytes 9437760 | tf_op jit(solution)/shard_map/gather | solution.py:84
  295.2 3.4 %copy.30 = bf16[144,2,64,128]{3,2,0,1:T(8,128)(2,1)S(1)} copy(bf16[144,2,64,128]{3,2,1,0:T(8,128)(2,1)} %gather_fusion.5) | data formatting | bytes 9437184 | tf_op jit(solution)/shard_map/gather | solution.py:84
  302.9 1.0 convert_add_fusion
  (118 shorter events, 21.1 us)
Async XLA Ops:
  0.6 20.5 %copy-start.10 = (f32[6,1,128,128]{3,2,1,0:T(8,128)S(1)}, f32[6,1,128,128]{3,2,1,0:T(8,128)}, u32[]{:S(2)}) copy-start(f32[6,1,128,128]{3,2,1,0:T(8,128)} %param.12) | copy-start | bytes 1179652
  0.6 21.2 %copy-start.28 = (s32[384]{0:T(512)S(1)}, s32[384]{0:T(512)}, u32[]{:S(2)}) copy-start(s32[384]{0:T(512)} %param.11) | copy-start | bytes 4612
  0.7 21.3 %copy-start.12 = (f32[3,1,128,128]{3,2,1,0:T(8,128)S(1)}, f32[3,1,128,128]{3,2,1,0:T(8,128)}, u32[]{:S(2)}) copy-start(f32[3,1,128,128]{3,2,1,0:T(8,128)} %param.13) | copy-start | bytes 589828
  2.7 128.4 %collective-permute-start = (bf16[2,384,128]{2,1,0:T(8,128)(2,1)}, bf16[2,384,128]{2,1,0:T(8,128)(2,1)}, u32[]{:S(2)}, u32[]{:S(2)}) collective-permute-start(bf16[2,384,128]{2,1,0:T(8,128)(2,1)} %get-tuple-element.18), channel_id=1, source_target_pairs={{0,1},{1,2},{2,3},{3,4},{4,5},{5,6},{6,7},{7,8},{8,9},{9,10},{10,1... | collective-permute-start | bytes 589832 | tf_op jit(solution)/shard_map/ppermute | solution.py:21
  5.8 125.3 %collective-permute-start.1 = (bf16[2,384,128]{2,1,0:T(8,128)(2,1)}, bf16[2,384,128]{2,1,0:T(8,128)(2,1)}, u32[]{:S(2)}, u32[]{:S(2)}) collective-permute-start(bf16[2,384,128]{2,1,0:T(8,128)(2,1)} %get-tuple-element.19), channel_id=1, source_target_pairs={{1,0},{2,1},{3,2},{4,3},{5,4},{6,5},{7,6},{8,7},{9,8},{10,9},{11,1... | collective-permute-start | bytes 589832 | tf_op jit(solution)/shard_map/ppermute | solution.py:24
  17.0 98.6 %collective-permute-start.6 = (bf16[2,1,128,128]{3,2,1,0:T(8,128)(2,1)}, bf16[2,1,128,128]{3,2,1,0:T(8,128)(2,1)}, u32[]{:S(2)}, u32[]{:S(2)}) collective-permute-start(bf16[2,1,128,128]{3,2,1,0:T(8,128)(2,1)} %slice.372), channel_id=1, source_target_pairs={{1,0},{2,1},{3,2},{4,3},{5,4},{6,5},{7,6},{8,7},{9,8},{10,9},{11,1... | collective-permute-start | bytes 196616 | tf_op jit(solution)/shard_map/ppermute | solution.py:32
  21.9 85.6 %copy-start.26 = (f32[3,384]{1,0:T(4,128)S(1)}, f32[3,384]{1,0:T(4,128)}, u32[]{:S(2)}) copy-start(f32[3,384]{1,0:T(4,128)} %param.10) | copy-start | bytes 13828
  21.9 85.9 %copy-start.27 = (s32[12,12]{1,0:T(8,128)S(1)}, s32[12,12]{1,0:T(8,128)}, u32[]{:S(2)}) copy-start(s32[12,12]{1,0:T(8,128)} %param.9) | copy-start | bytes 1732
  109.7 6.0 %copy-start.21 = (f32[12,12,3]{1,0,2:T(8,128)}, f32[12,12,3]{1,0,2:T(8,128)S(1)}, u32[]{:S(2)}) copy-start(f32[12,12,3]{1,0,2:T(8,128)S(1)} %reshape.332) | copy-start | bytes 5188
  109.9 6.6 %copy-start.18 = (f32[1,128,128]{2,1,0:T(8,128)S(1)}, f32[1,128,128]{2,1,0:T(8,128)}, u32[]{:S(2)}) copy-start(f32[1,128,128]{2,1,0:T(8,128)} %get-tuple-element.11) | copy-start | bytes 196612
  109.9 6.6 %copy-start.19 = (f32[1,128,128]{2,1,0:T(8,128)S(1)}, f32[1,128,128]{2,1,0:T(8,128)}, u32[]{:S(2)}) copy-start(f32[1,128,128]{2,1,0:T(8,128)} %get-tuple-element.12) | copy-start | bytes 196612
  109.9 6.6 %copy-start.20 = (f32[1,128,128]{2,1,0:T(8,128)S(1)}, f32[1,128,128]{2,1,0:T(8,128)}, u32[]{:S(2)}) copy-start(f32[1,128,128]{2,1,0:T(8,128)} %get-tuple-element.13) | copy-start | bytes 196612
  116.7 14.4 %copy-start.3 = (f32[3,1,128,128]{3,2,1,0:T(8,128)}, f32[3,1,128,128]{3,2,1,0:T(8,128)S(1)}, u32[]{:S(2)}) copy-start(f32[3,1,128,128]{3,2,1,0:T(8,128)S(1)} %fusion.46) | copy-start | bytes 589828
  116.8 13.6 %collective-permute-start.7 = (bf16[2,1,128,128]{3,2,1,0:T(8,128)(2,1)S(1)}, bf16[2,1,128,128]{3,2,1,0:T(8,128)(2,1)S(1)}, u32[]{:S(2)}, u32[]{:S(2)}) collective-permute-start(bf16[2,1,128,128]{3,2,1,0:T(8,128)(2,1)S(1)} %slice.371), channel_id=1, source_target_pairs={{0,1},{1,2},{2,3},{3,4},{4,5},{5,6},{6,7},{7,8},{8,9},{9,10},{10,1... | collective-permute-start | bytes 196616 | tf_op jit(solution)/shard_map/ppermute | solution.py:32
  139.7 3.6 %copy-start = (bf16[12,12,64,64]{3,2,1,0:T(8,128)(2,1)S(1)}, bf16[12,12,64,64]{3,2,1,0:T(8,128)(2,1)}, u32[]{:S(2)}) copy-start(bf16[12,12,64,64]{3,2,1,0:T(8,128)(2,1)} %get-tuple-element.6) | copy-start | bytes 3538948
  146.8 1.6 copy-start.24
  148.4 1.7 copy-start.22
  151.0 99.3 %collective-permute-start.2 = (bf16[2,384,128]{2,1,0:T(8,128)(2,1)}, bf16[2,384,128]{2,1,0:T(8,128)(2,1)S(1)}, u32[]{:S(2)}, u32[]{:S(2)}) collective-permute-start(bf16[2,384,128]{2,1,0:T(8,128)(2,1)} %get-tuple-element.16), channel_id=1, source_target_pairs={{0,1},{1,2},{2,3},{3,4},{4,5},{5,6},{6,7},{7,8},{8,9},{9,10},{10,1... | collective-permute-start | bytes 589832 | tf_op jit(solution)/shard_map/ppermute | solution.py:21
  153.0 98.1 %collective-permute-start.3 = (bf16[2,384,128]{2,1,0:T(8,128)(2,1)S(1)}, bf16[2,384,128]{2,1,0:T(8,128)(2,1)}, u32[]{:S(2)}, u32[]{:S(2)}) collective-permute-start(bf16[2,384,128]{2,1,0:T(8,128)(2,1)S(1)} %get-tuple-element.17), channel_id=1, source_target_pairs={{1,0},{2,1},{3,2},{4,3},{5,4},{6,5},{7,6},{8,7},{9,8},{10,9},{11,1... | collective-permute-start | bytes 589832 | tf_op jit(solution)/shard_map/ppermute | solution.py:24
  263.1 1.7 copy-start.1
  266.2 21.4 %copy-start.6 = (bf16[12,64,128]{2,1,0:T(8,128)(2,1)}, bf16[12,64,128]{2,1,0:T(8,128)(2,1)S(1)}, u32[]{:S(2)}) copy-start(bf16[12,64,128]{2,1,0:T(8,128)(2,1)S(1)} %fusion.38) | copy-start | bytes 589828
  266.2 13.3 %copy-start.11 = (f32[6,1,128,128]{3,2,1,0:T(8,128)S(1)}, f32[6,1,128,128]{3,2,1,0:T(8,128)}, u32[]{:S(2)}) copy-start(f32[6,1,128,128]{3,2,1,0:T(8,128)} %param.12) | copy-start | bytes 1179652
  266.2 13.3 %copy-start.13 = (f32[3,1,128,128]{3,2,1,0:T(8,128)S(1)}, f32[3,1,128,128]{3,2,1,0:T(8,128)}, u32[]{:S(2)}) copy-start(f32[3,1,128,128]{3,2,1,0:T(8,128)} %param.13) | copy-start | bytes 589828
  266.2 13.3 %copy-start.14 = (f32[3,1,128,128]{3,2,1,0:T(8,128)S(1)}, f32[3,1,128,128]{3,2,1,0:T(8,128)}, u32[]{:S(2)}) copy-start(f32[3,1,128,128]{3,2,1,0:T(8,128)} %copy.32) | copy-start | bytes 589828
  266.2 13.3 %copy-start.15 = (f32[1,1,128,128]{3,2,1,0:T(8,128)S(1)}, f32[1,1,128,128]{3,2,1,0:T(8,128)}, u32[]{:S(2)}) copy-start(f32[1,1,128,128]{3,2,1,0:T(8,128)} %fusion.58) | copy-start | bytes 196612
  266.2 13.3 %copy-start.16 = (f32[1,1,128,128]{3,2,1,0:T(8,128)S(1)}, f32[1,1,128,128]{3,2,1,0:T(8,128)}, u32[]{:S(2)}) copy-start(f32[1,1,128,128]{3,2,1,0:T(8,128)} %get-tuple-element.20) | copy-start | bytes 196612
  266.2 13.3 %copy-start.17 = (f32[1,1,128,128]{3,2,1,0:T(8,128)S(1)}, f32[1,1,128,128]{3,2,1,0:T(8,128)}, u32[]{:S(2)}) copy-start(f32[1,1,128,128]{3,2,1,0:T(8,128)} %get-tuple-element.21) | copy-start | bytes 196612
  266.3 14.0 %copy-start.4 = (f32[3,1,128,128]{3,2,1,0:T(8,128)S(1)}, f32[3,1,128,128]{3,2,1,0:T(8,128)}, u32[]{:S(2)}) copy-start(f32[3,1,128,128]{3,2,1,0:T(8,128)} %copy-done.3) | copy-start | bytes 589828
  267.0 20.7 %copy-start.8 = (bf16[12,64,128]{2,1,0:T(8,128)(2,1)}, bf16[12,64,128]{2,1,0:T(8,128)(2,1)S(1)}, u32[]{:S(2)}) copy-start(bf16[12,64,128]{2,1,0:T(8,128)(2,1)S(1)} %fusion.39) | copy-start | bytes 589828
  267.0 19.5 %collective-permute-start.4 = (bf16[2,384,128]{2,1,0:T(8,128)(2,1)S(1)}, bf16[2,384,128]{2,1,0:T(8,128)(2,1)S(1)}, u32[]{:S(2)}, u32[]{:S(2)}) collective-permute-start(bf16[2,384,128]{2,1,0:T(8,128)(2,1)S(1)} %get-tuple-element.14), channel_id=1, source_target_pairs={{0,1},{1,2},{2,3},{3,4},{4,5},{5,6},{6,7},{7,8},{8,9},{9,10},{10,1... | collective-permute-start | bytes 589832 | tf_op jit(solution)/shard_map/ppermute | solution.py:21
  269.5 18.1 %collective-permute-start.5 = (bf16[2,384,128]{2,1,0:T(8,128)(2,1)S(1)}, bf16[2,384,128]{2,1,0:T(8,128)(2,1)S(1)}, u32[]{:S(2)}, u32[]{:S(2)}) collective-permute-start(bf16[2,384,128]{2,1,0:T(8,128)(2,1)S(1)} %get-tuple-element.15), channel_id=1, source_target_pairs={{1,0},{2,1},{3,2},{4,3},{5,4},{6,5},{7,6},{8,7},{9,8},{10,9},{11,1... | collective-permute-start | bytes 589832 | tf_op jit(solution)/shard_map/ppermute | solution.py:24
  298.7 1.7 copy-start.2
  (5 other events, 5.2 us)
where the time goes:
time: 309 us; the launch traced here: 304 us
  blocking collectives  152 us (49%)
  local copies, waits for them, and re-layouts  57.6 us (19%)
  starting transfers between devices  42.9 us (14%)
  other arithmetic  21.1 us (7%)
  waiting for transfers between devices  17.3 us (6%)
  matrix products  12.2 us (4%)
    psum x1, blocking collectives, body(): at_atoms = lax.psum(looked, ('grp', 'row'))  76.3 us
    psum x1, blocking collectives, body(): current = lax.psum(spread, ('grp', 'row'))  75.3 us
    gather x6, local copies, waits for them, and re-layouts, apply_blocks(): picked = extended[:, local_cols]  33.1 us
    ppermute x3, starting transfers between devices, with_halo(): lax.ppermute(lax.slice_in_dim(block, 0, width, axis=dim), axis, backward)  30 us
    ppermute x2, waiting for transfers between devices, from_behind(): lax.ppermute(value, axis, [(source, source + steps) for source in range(l...  10.8 us
    unnamed x60, local copies, waits for them, and re-layouts  8.07 us
    ppermute x3, starting transfers between devices, with_halo(): lax.ppermute(lax.slice_in_dim(block, block.shape[dim] - width, None, axis...  7.47 us
  transfers between devices with their start and end apart: 8, of which 3 were waited for; matrix products, arithmetic and copies ran while one was open for 12% of the time, Pallas kernels for 0%

commit v1 on v0

v1 whole, which is shorter than its diff:
```python
import functools
import math

import jax
import jax.numpy as jnp
from jax import lax
from jax.experimental import pallas as pl
from jax.experimental.pallas import tpu as pltpu
from jax.sharding import PartitionSpec as P

TERMS = 3
CHUNKS = 2

coupling = 0.7
elec_step = 1.5
wave_step = 0.5

MESH = pl.DeviceIdType.MESH
F32 = jnp.float32
BF16 = jnp.bfloat16


def iota(shape, dim):
    return lax.broadcasted_iota(jnp.int32, shape, dim)


def shifted(value, dim, forward):
    extent = value.shape[dim]
    moved = pltpu.roll(value, extent - 1 if forward else 1, dim)
    rim = extent - 1 if forward else 0
    return jnp.where(iota(value.shape, dim) == rim, 0.0, moved)


def kernel(
    groups, rows,
    coef_hbm, ham_hbm, nbr, pos, site, field_hbm, pot_hbm,
    coef_out, field_out, pot_out,
    ham, placed, turned, phased, own, vp, halo, weights, inner,
    field, pot, e_send, e_recv, b_send, b_recv,
    at_send, at_recv, cur_send, cur_recv, posb, cos_tab, sin_tab, share,
    in_sem, at_ss, at_rs, cur_ss, cur_rs, t_ss, t_rs, rim_ss, rim_rs,
):
    atoms = nbr.shape[0]
    blocks = nbr.shape[1]
    reach = atoms // 2
    orb = ham.shape[2]
    lanes = 2 * orb
    pairs = atoms // 2
    wide = 2 * reach + 2
    half_rows = reach * orb
    own_rows = atoms * orb
    atoms_all = pos.shape[1]
    planes = groups * rows
    per_row = planes // rows
    sources = 2 * per_row

    g = lax.axis_index("grp")
    r = lax.axis_index("row")
    s = g * rows + r
    q = lax.div(s, per_row)
    m = lax.rem(s, per_row)
    near = m < per_row // 2
    other = jnp.where(near, q - 1, q + 1)
    other_ok = (other >= 0) & (other < rows)

    def owner(p):
        return lax.div(p, rows), lax.rem(p, rows)

    def device(gg, rr):
        return {"grp": gg, "row": rr}

    next_g, next_r = owner(jnp.minimum(s + 1, planes - 1))
    prev_g, prev_r = owner(jnp.maximum(s - 1, 0))
    has_next, has_prev = s < planes - 1, s > 0
    has_up, has_down = r < rows - 1, r > 0

    loads = [
        pltpu.make_async_copy(pot_hbm, pot, in_sem.at[0]),
        pltpu.make_async_copy(coef_hbm, coef_out, in_sem.at[1]),
        pltpu.make_async_copy(ham_hbm, ham, in_sem.at[2]),
        pltpu.make_async_copy(field_hbm, field, in_sem.at[3]),
    ]
    for load in loads:
        load.start()

    barrier = pltpu.get_barrier_semaphore()

    def tell(gg, rr):
        pl.semaphore_signal(barrier, inc=1, device_id=device(gg, rr), device_id_type=MESH)

    first_plane = per_row * r - per_row // 2

    def tell_sources(i, carry):
        p = first_plane + i
        gg, rr = owner(jnp.clip(p, 0, planes - 1))

        @pl.when((p >= 0) & (p < planes) & ((gg != g) | (rr != r)))
        def _():
            tell(gg, rr)

        return carry

    def tell_currents(gg, carry):
        @pl.when((gg != g) | (q != r))
        def _():
            tell(gg, q)

        return carry

    @pl.when(has_next)
    def _():
        tell(next_g, next_r)

    @pl.when(has_prev)
    def _():
        tell(prev_g, prev_r)

    lax.fori_loop(0, sources, tell_sources, 0)
    lax.fori_loop(0, groups, tell_currents, 0)

    first_here = lax.div(3 * s + 1, 2)
    second_ok = lax.rem(s, 2) == 0
    second_here = jnp.minimum(first_here + 1, atoms_all - 1)
    site_one = site[first_here]
    site_two = jnp.where(second_ok, site[second_here], -1)
    grid_y, grid_z = pot.shape[1], pot.shape[2]
    cell = iota((grid_y, grid_z), 0) * grid_z + iota((grid_y, grid_z), 1)
    at_one = cell == site_one
    at_two = cell == site_two
    tile = (8, 128)
    sub8, lane8 = iota(tile, 0), iota(tile, 1)

    loads[0].wait()
    found = []
    for mask in (at_one, at_two):
        for c in range(3):
            hit = jnp.sum(jnp.where(mask, pot[c], 0.0), axis=0, keepdims=True)
            found.append(jnp.sum(hit, axis=1, keepdims=True))
    for k, target in enumerate((q, other)):
        lane_one = first_here - atoms * target + reach
        message = jnp.zeros(tile, F32)
        for j in range(2):
            for c in range(3):
                message = message + jnp.where(
                    (sub8 == c) & (lane8 == lane_one + j), found[3 * j + c], 0.0
                )
        at_send[k] = message

    low_lanes = iota((orb, lanes), 1) < orb
    half = lanes // 2

    def turn(value):
        return pltpu.roll(value, half, 1)

    loads[1].wait()

    def pack(a, carry):
        at = pl.ds(pl.multiple_of(a * orb, orb), orb)
        real = coef_out[0, at, :]
        imag = coef_out[1, at, :]
        real_turned, imag_turned = turn(real), turn(imag)
        first = jnp.where(low_lanes, real, imag_turned)
        first_other = jnp.where(low_lanes, -imag, real_turned)
        second = jnp.where(low_lanes, real_turned, imag)
        second_other = jnp.where(low_lanes, -imag_turned, real)
        for c, (value, rotated) in enumerate(((first, first_other), (second, second_other))):
            value = value.astype(BF16)
            rotated = rotated.astype(BF16)
            own[0, c, at, :] = value
            vp[c, at, :] = rotated
            base = pl.multiple_of((a + reach) * lanes, lanes)
            weights[0, c, pl.ds(base, orb), :] = value
            weights[0, c, pl.ds(base + orb, orb), :] = rotated
        return carry

    lax.fori_loop(0, atoms, pack, 0)

    loads[3].wait()
    for c in range(2):
        e_send[c] = field[1 + c].astype(BF16)

    def ones(cond):
        return jnp.where(cond, 1, 0)

    expected = (
        2 * groups
        + groups * ones(other_ok)
        - 2 * ones(q == r)
        - ones(other_ok & (other == r))
        + ones(has_next)
        + ones(has_prev)
    )
    pl.semaphore_wait(barrier, expected)

    def at_copy(k, slot, gg, rr):
        return pltpu.make_async_remote_copy(
            src_ref=at_send.at[k], dst_ref=at_recv.at[slot],
            send_sem=at_ss.at[k, gg], recv_sem=at_rs.at[slot],
            device_id=device(gg, rr), device_id_type=MESH,
        )

    slot_own = m + per_row // 2
    slot_other = jnp.where(near, m + per_row + per_row // 2, m - per_row // 2)

    def for_at_sends(action, keep):
        for k, (target, slot, ok) in enumerate(
            ((q, slot_own, None), (other, slot_other, other_ok))
        ):
            def one(gg, carry, k=k, target=target, slot=slot, ok=ok):
                is_self = (gg == g) & (target == r)
                go = jnp.logical_not(is_self)
                if ok is not None:
                    go = go & ok

                @pl.when(go)
                def _():
                    action(at_copy(k, slot, gg, target))

                if keep:
                    @pl.when(is_self)
                    def _():
                        at_recv[slot] = at_send[k]

                return carry

            lax.fori_loop(0, groups, one, 0)

    for_at_sends(lambda copy: copy.start(), True)

    def t_copy(k, c, up):
        side = 0 if up else 1
        source = pl.ds(own_rows - half_rows, half_rows) if up else pl.ds(0, half_rows)
        rr = next_r if up else prev_r
        return pltpu.make_async_remote_copy(
            src_ref=own.at[k, c, source, :], dst_ref=halo.at[k, c, side],
            send_sem=t_ss.at[k, c, side], recv_sem=t_rs.at[k, c, side],
            device_id=device(g, rr), device_id_type=MESH,
        )

    def send_term(k, c):
        @pl.when(has_up)
        def _():
            t_copy(k, c, True).start()

        @pl.when(has_down)
        def _():
            t_copy(k, c, False).start()

    for c in range(CHUNKS):
        send_term(0, c)

    e_copy = pltpu.make_async_remote_copy(
        src_ref=e_send, dst_ref=e_recv, send_sem=rim_ss.at[0], recv_sem=rim_rs.at[0],
        device_id=device(prev_g, prev_r), device_id_type=MESH,
    )
    b_copy = pltpu.make_async_remote_copy(
        src_ref=b_send, dst_ref=b_recv, send_sem=rim_ss.at[1], recv_sem=rim_rs.at[1],
        device_id=device(next_g, next_r), device_id_type=MESH,
    )

    @pl.when(has_prev)
    def _():
        e_copy.start()

    loads[2].wait()
    zero_block = jnp.zeros((orb, lanes), F32)
    chunk_rows = 16

    def place(a, carry):
        i = lax.div(a, 2)
        odd = lax.rem(a, 2)
        offsets = [nbr[a, n] - atoms * r - a + reach for n in range(blocks)]

        def piece(part, inner_carry):
            at = pl.multiple_of(part * chunk_rows, chunk_rows)
            to = pl.ds(pl.multiple_of(odd * orb + at, chunk_rows), chunk_rows)
            held = [ham[a, n, pl.ds(at, chunk_rows), :].astype(F32) for n in range(blocks)]
            for d in range(wide - 1):
                who = list(range(3, blocks))
                if d == reach:
                    who = [0] + who
                if d == 0 or d == 2 * reach:
                    who = [1, 2] + who
                total = None
                for n in who:
                    scale = jnp.where(offsets[n] == d, 1.0, 0.0).astype(F32)
                    part_sum = held[n] * scale
                    total = part_sum if total is None else total + part_sum
                lane_at = pl.ds(pl.multiple_of((d + odd) * lanes, lanes), lanes)
                placed[i, to, lane_at] = total
                turned[i, to, lane_at] = turn(total)
            return inner_carry

        lax.fori_loop(0, orb // chunk_rows, piece, 0)
        return carry

    lax.fori_loop(0, atoms, place, 0)
    for i in range(pairs):
        phased[i, 0:orb, (wide - 1) * lanes : wide * lanes] = zero_block.astype(BF16)
        phased[i, orb : 2 * orb, 0:lanes] = zero_block.astype(BF16)

    posb[...] = jnp.zeros(posb.shape, F32)
    posb[0:3, 0:atoms_all] = pos[...]
    shift = lax.rem(2 * posb.shape[1] + reach - atoms * r, posb.shape[1])
    near_pos = pltpu.roll(posb[...], shift, 1)[:, 0:128]
    sub16, lane16 = iota((16, 128), 0), iota((16, 128), 1)

    def column(row, step, offset):
        return jnp.sum(
            jnp.where(lane16 == step * sub16 + offset, row, 0.0), axis=1, keepdims=True
        )

    pos_rows = [near_pos[c : c + 1, :] for c in range(3)]
    pos_cols = [column(row, 1, reach) for row in pos_rows]

    def at_source(i):
        p = first_plane + i
        gg, rr = owner(jnp.clip(p, 0, planes - 1))
        return (p >= 0) & (p < planes), (gg == g) & (rr == r), gg, rr

    def at_wait(i, total):
        ok, is_self, gg, rr = at_source(i)

        @pl.when(ok & jnp.logical_not(is_self))
        def _():
            at_copy(0, i, gg, rr).wait_recv()

        return total

    lax.fori_loop(0, sources, at_wait, 0)
    at_near = jnp.zeros(tile, F32)
    for i in range(sources):
        ok = at_source(i)[0]
        at_near = at_near + jnp.where(ok, at_recv[i], 0.0)

    angle = jnp.zeros((16, 128), F32)
    for c in range(3):
        row = at_near[c : c + 1, :]
        angle = angle + 0.5 * (column(row, 1, reach) + row) * (pos_rows[c] - pos_cols[c])
    angle = coupling * angle
    cosine, sine = jnp.cos(angle), jnp.sin(angle)
    for i in range(pairs):
        back = (128 - 2 * i) % 128
        c_rows, s_rows = cosine, sine
        if back:
            c_rows, s_rows = pltpu.roll(cosine, back, 1), pltpu.roll(sine, back, 1)
        cos_tab[2 * i : 2 * i + 2, :] = c_rows[2 * i : 2 * i + 2, :]
        sin_tab[2 * i : 2 * i + 2, :] = s_rows[2 * i : 2 * i + 2, :]

    signs = jnp.where(iota((1, lanes), 1) < orb, -1.0, 1.0).astype(F32)

    def phase(i, carry):
        for odd in range(2):
            c_row = cos_tab[pl.ds(2 * i + odd, 1), :]
            s_row = sin_tab[pl.ds(2 * i + odd, 1), :]
            at = slice(odd * orb, (odd + 1) * orb)
            for d in range(odd, wide - 1 + odd):
                lane_at = slice(d * lanes, (d + 1) * lanes)
                c_here = jnp.broadcast_to(c_row[:, d : d + 1], (orb, lanes))
                s_here = jnp.broadcast_to(s_row[:, d : d + 1], (1, lanes)) * signs
                phased[i, at, lane_at] = (
                    placed[i, at, lane_at] * c_here + turned[i, at, lane_at] * s_here
                ).astype(BF16)
        return carry

    lax.fori_loop(0, pairs, phase, 0)

    out_signs = -signs
    inner_at, inner_end = reach, reach + atoms

    def dot(left, right):
        return jnp.dot(left, right, preferred_element_type=F32)

    def inner_products(k, c):
        par = k % 2
        for i in range(pairs):
            low, high = max(2 * i, inner_at), min(2 * i + wide, inner_end)
            inner[c, i * lanes : (i + 1) * lanes, :] = dot(
                phased[i, :, (low - 2 * i) * lanes : (high - 2 * i) * lanes],
                weights[par, c, low * lanes : high * lanes, :],
            )

    def take_halo(k, c, up_side):
        par = k % 2
        side = 1 if up_side else 0
        ok = has_up if up_side else has_down

        @pl.when(ok)
        def _():
            t_copy(k, c, not up_side).wait_recv()

        first = inner_end if up_side else 0
        for j in range(reach):
            value = halo[k, c, side, j * orb : (j + 1) * orb, :].astype(F32)
            value = jnp.where(ok, value, 0.0)
            base = (first + j) * lanes
            weights[par, c, base : base + orb, :] = value.astype(BF16)
            weights[par, c, base + orb : base + lanes, :] = (turn(value) * signs).astype(BF16)

    def finish_term(k, c):
        par = k % 2
        factor = elec_step / (k + 1)
        for up_side in (False, True):
            take_halo(k, c, up_side)
            for i in range(pairs // 2):
                if up_side:
                    i = i + pairs // 2
                    low, high = inner_end, 2 * i + wide
                else:
                    low, high = 2 * i, inner_at
                at = slice(i * lanes, (i + 1) * lanes)
                product = factor * (
                    inner[c, at, :]
                    + dot(
                        phased[i, :, (low - 2 * i) * lanes : (high - 2 * i) * lanes],
                        weights[par, c, low * lanes : high * lanes, :],
                    )
                )
                rotated = product.astype(BF16)
                value = (turn(product) * out_signs).astype(BF16)
                own[k + 1, c, at, :] = value
                if k + 1 < TERMS:
                    for j in range(2):
                        base = (inner_at + 2 * i + j) * lanes
                        part = slice(j * orb, (j + 1) * orb)
                        weights[1 - par, c, base : base + orb, :] = value[part]
                        weights[1 - par, c, base + orb : base + lanes, :] = rotated[part]

    def add_terms(which):
        def one(a, carry):
            at = pl.ds(pl.multiple_of(a * orb, orb), orb)
            first = sum(own[k, 0, at, :].astype(F32) for k in which)
            second = sum(own[k, 1, at, :].astype(F32) for k in which)
            coef_out[0, at, :] = coef_out[0, at, :] + jnp.where(low_lanes, first, turn(second))
            coef_out[1, at, :] = coef_out[1, at, :] + jnp.where(low_lanes, turn(first), second)
            return carry

        lax.fori_loop(0, atoms, one, 0)

    for c in range(CHUNKS):
        inner_products(0, c)
    for c in range(CHUNKS):
        finish_term(0, c)
        send_term(1, c)

    @pl.when(has_prev)
    def _():
        e_copy.wait_send()

    @pl.when(has_next)
    def _():
        e_copy.wait_recv()

    comp = [field[c] for c in range(3)]
    ahead = [jnp.where(has_next, e_recv[c].astype(F32), 0.0) for c in range(2)]

    def ahead_y(v):
        return shifted(v, 0, True) - v

    def ahead_z(v):
        return shifted(v, 1, True) - v

    curl = (
        ahead_y(comp[2]) - ahead_z(comp[1]),
        ahead_z(comp[0]) - (ahead[1] - comp[2]),
        (ahead[0] - comp[1]) - ahead_y(comp[0]),
    )
    for c in range(3):
        field_out[3 + c] = field[3 + c] - wave_step * curl[c]
    for c in range(2):
        b_send[c] = field_out[4 + c].astype(BF16)

    @pl.when(has_next)
    def _():
        b_copy.start()

    for c in range(CHUNKS):
        inner_products(1, c)

    def shares(i, carry):
        left = [vp[c, pl.ds(pl.multiple_of(i * lanes, lanes), lanes), :] for c in range(CHUNKS)]
        for d in range(0, wide, 2):
            base = pl.multiple_of(i * 2 * lanes + d * lanes, 2 * lanes)
            rows_at = pl.ds(base, 2 * lanes)
            gram = None
            for c in range(CHUNKS):
                product = lax.dot_general(
                    left[c], weights[0, c, rows_at, :], (((1,), (1,)), ((), ())),
                    preferred_element_type=F32,
                )
                gram = product if gram is None else gram + product
            gram = gram * phased[i, :, d * lanes : (d + 2) * lanes].astype(F32)
            for odd in range(2):
                summed = jnp.sum(gram[odd * orb : (odd + 1) * orb], axis=0, keepdims=True)
                for j in range(2):
                    share[2 * i + odd, d + j : d + j + 1, :] = summed[
                        :, j * lanes : (j + 1) * lanes
                    ]
        return carry

    share[...] = jnp.zeros(share.shape, F32)
    lax.fori_loop(0, pairs, shares, 0)
    scale = 1.0 / math.sqrt(2.0 * orb * groups * lanes)
    for a in range(16):
        if a >= atoms:
            cur_send[a : a + 1, :] = jnp.zeros((1, 128), F32)
            continue
        each = jnp.sum(share[a], axis=1, keepdims=True)
        line = jnp.zeros((1, 128), F32)
        for c in range(3):
            bond = column(pos_rows[c], 1, 2 * (a // 2)) - pos_cols[c][a : a + 1, :]
            value = scale * jnp.sum(each * bond, axis=0, keepdims=True)
            line = line + jnp.where(iota((1, 128), 1) == c, value, 0.0)
        cur_send[a : a + 1, :] = line

    def cur_copy(i, slot, gg, rr):
        return pltpu.make_async_remote_copy(
            src_ref=cur_send, dst_ref=cur_recv.at[slot],
            send_sem=cur_ss.at[i], recv_sem=cur_rs.at[slot],
            device_id=device(gg, rr), device_id_type=MESH,
        )

    def for_cur_sends(action, keep):
        def one(i, carry):
            gg, rr = owner(per_row * r + i)
            is_self = (gg == g) & (rr == r)

            @pl.when(jnp.logical_not(is_self))
            def _():
                action(cur_copy(i, g, gg, rr))

            if keep:
                @pl.when(is_self)
                def _():
                    cur_recv[g] = cur_send[...]

            return carry

        lax.fori_loop(0, per_row, one, 0)

    for_cur_sends(lambda copy: copy.start(), True)

    for c in range(CHUNKS):
        finish_term(1, c)
        send_term(2, c)
    for c in range(CHUNKS):
        inner_products(2, c)
    add_terms((1, 2))

    @pl.when(has_next)
    def _():
        b_copy.wait_send()

    @pl.when(has_prev)
    def _():
        b_copy.wait_recv()

    def cur_wait(gg, carry):
        @pl.when((gg != g) | (q != r))
        def _():
            cur_copy(0, gg, gg, q).wait_recv()

        return carry

    lax.fori_loop(0, groups, cur_wait, 0)
    current = cur_recv[0]
    for gg in range(1, groups):
        current = current + cur_recv[gg]
    atom_one = first_here - atoms * q

    def picked(atom, c):
        hit = jnp.where((sub16 == atom) & (lane16 == c), current, 0.0)
        return jnp.sum(jnp.sum(hit, axis=0, keepdims=True), axis=1, keepdims=True)

    comp = [field_out[3 + c] for c in range(3)]
    behind = [jnp.where(has_prev, b_recv[c].astype(F32), 0.0) for c in range(2)]

    def behind_y(v):
        return v - shifted(v, 0, False)

    def behind_z(v):
        return v - shifted(v, 1, False)

    curl = (
        behind_y(comp[2]) - behind_z(comp[1]),
        behind_z(comp[0]) - (comp[2] - behind[1]),
        (comp[1] - behind[0]) - behind_y(comp[0]),
    )
    for c in range(3):
        source = jnp.where(at_one, picked(atom_one, c), 0.0) + jnp.where(
            at_two, picked(atom_one + 1, c), 0.0
        )
        electric = field[c] + wave_step * (curl[c] - source)
        field_out[c] = electric
        pot_out[c] = pot[c] - wave_step * electric

    for c in range(CHUNKS):
        finish_term(2, c)
    add_terms((3,))

    for_at_sends(lambda copy: copy.wait_send(), False)
    for_cur_sends(lambda copy: copy.wait_send(), False)
    for k in range(TERMS):
        for c in range(CHUNKS):
            @pl.when(has_up)
            def _():
                t_copy(k, c, True).wait_send()

            @pl.when(has_down)
            def _():
                t_copy(k, c, False).wait_send()


def body(groups, rows, coefficients, hamiltonian, neighbours, positions, atom_site, rs_field, potential):
    atoms, blocks, orb = hamiltonian.shape[:3]
    lanes = 2 * orb
    reach = atoms // 2
    pairs = atoms // 2
    wide = 2 * reach + 2
    per_row = groups
    grid = rs_field.shape[2:]
    own_rows = atoms * orb
    field_in = rs_field.reshape((6,) + grid)
    pot_in = potential.reshape((3,) + grid)
    dma = pltpu.SemaphoreType.DMA
    vmem = pl.BlockSpec(memory_space=pltpu.VMEM)
    smem = pl.BlockSpec(memory_space=pltpu.SMEM)
    hbm = pl.BlockSpec(memory_space=pl.ANY)
    coef, field, pot = pl.pallas_call(
        functools.partial(kernel, groups, rows),
        out_shape=(
            jax.ShapeDtypeStruct(coefficients.shape, F32),
            jax.ShapeDtypeStruct(field_in.shape, F32),
            jax.ShapeDtypeStruct(pot_in.shape, F32),
        ),
        in_specs=[hbm, hbm, smem, vmem, smem, hbm, hbm],
        out_specs=(vmem, vmem, vmem),
        scratch_shapes=[
            pltpu.VMEM(hamiltonian.shape, BF16),
            pltpu.VMEM((pairs, 2 * orb, wide * lanes), F32),
            pltpu.VMEM((pairs, 2 * orb, wide * lanes), F32),
            pltpu.VMEM((pairs, 2 * orb, wide * lanes), BF16),
            pltpu.VMEM((TERMS + 1, CHUNKS, own_rows, lanes), BF16),
            pltpu.VMEM((CHUNKS, own_rows, lanes), BF16),
            pltpu.VMEM((TERMS, CHUNKS, 2, reach * orb, lanes), BF16),
            pltpu.VMEM((2, CHUNKS, (atoms + 2 * reach) * lanes, lanes), BF16),
            pltpu.VMEM((CHUNKS, own_rows, lanes), F32),
            pltpu.VMEM(field_in.shape, F32),
            pltpu.VMEM(pot_in.shape, F32),
            pltpu.VMEM((2,) + grid, BF16),
            pltpu.VMEM((2,) + grid, BF16),
            pltpu.VMEM((2,) + grid, BF16),
            pltpu.VMEM((2,) + grid, BF16),
            pltpu.VMEM((2, 8, 128), F32),
            pltpu.VMEM((2 * per_row, 8, 128), F32),
            pltpu.VMEM((16, 128), F32),
            pltpu.VMEM((groups, 16, 128), F32),
            pltpu.VMEM((8, 512), F32),
            pltpu.VMEM((16, 128), F32),
            pltpu.VMEM((16, 128), F32),
            pltpu.VMEM((atoms, 16, 128), F32),
            dma((4,)),
            dma((2, groups)),
            dma((2 * per_row,)),
            dma((per_row,)),
            dma((groups,)),
            dma((TERMS, CHUNKS, 2)),
            dma((TERMS, CHUNKS, 2)),
            dma((2,)),
            dma((2,)),
        ],
        compiler_params=pltpu.CompilerParams(
            collective_id=0, has_side_effects=True, vmem_limit_bytes=48 * 2**20
        ),
    )(coefficients, hamiltonian, neighbours, positions, atom_site, field_in, pot_in)
    return coef, field.reshape(rs_field.shape), pot.reshape(potential.shape)


def solution(mesh):
    placed = (
        P(None, "row", "grp"),
        P("row", None, None, None),
        P("row", None),
        P(),
        P(),
        P(None, ("grp", "row"), None, None),
        P(None, ("grp", "row"), None, None),
    )
    return jax.shard_map(
        functools.partial(body, mesh.shape["grp"], mesh.shape["row"]),
        mesh=mesh,
        in_specs=placed,
        out_specs=(
            P(None, "row", "grp"),
            P(None, ("grp", "row"), None, None),
            P(None, ("grp", "row"), None, None),
        ),
        check_vma=False,
    )
```

time: 309 us -> 69.2 us (0.22)
  the two profiles are of different devices: /device:TPU:17 before, /device:TPU:94 now
where the time goes in v1:
time: 69.2 us; the launch traced here: 68.9 us
  Pallas kernels  59.2 us (86%)
  local copies, waits for them, and re-layouts  9.08 us (13%)
    pallas_call x1, Pallas kernels, body(): pl.pallas_call(functools.partial(kernel, groups, rows), out_shape=(jax.Sh...  59.2 us
    unnamed x17, local copies, waits for them, and re-layouts  9.08 us

profile of v1, /device:TPU:94, one launch (start us, length us, event | category | flops | bytes accessed | tf_op | source)
XLA Modules:
  0.0 68.9 jit_solution(1630375262447552554)
XLA Ops:
  0.6 0.0 copy-start
  0.6 1.7 %copy-done = bf16[12,12,64,128]{3,2,1,0:T(8,128)(2,1)S(1)} copy-done((bf16[12,12,64,128]{3,2,1,0:T(8,128)(2,1)S(1)}, bf16[12,12,64,128]{3,2,1,0:T(8,128)(2,1)}, u32[]{:S(2)}) %copy-start) | copy-done | bytes 2359320
  2.3 0.0 copy-start.1
  2.3 1.1 %copy-done.1 = f32[2,768,128]{2,1,0:T(8,128)S(1)} copy-done((f32[2,768,128]{2,1,0:T(8,128)S(1)}, f32[2,768,128]{2,1,0:T(8,128)}, u32[]{:S(2)}) %copy-start.1) | copy-done | bytes 786456
  3.4 0.0 copy-start.2
  3.4 1.0 %copy-done.2 = f32[6,1,128,128]{3,2,1,0:T(8,128)S(1)} copy-done((f32[6,1,128,128]{3,2,1,0:T(8,128)S(1)}, f32[6,1,128,128]{3,2,1,0:T(8,128)}, u32[]{:S(2)}) %copy-start.2) | copy-done | bytes 393240
  4.4 0.0 copy-start.3
  4.4 0.9 %copy-done.3 = f32[3,1,128,128]{3,2,1,0:T(8,128)S(1)} copy-done((f32[3,1,128,128]{3,2,1,0:T(8,128)S(1)}, f32[3,1,128,128]{3,2,1,0:T(8,128)}, u32[]{:S(2)}) %copy-start.3) | copy-done | bytes 196632
  5.4 0.0 copy-start.4
  5.4 0.7 %copy-done.4 = s32[12,12]{1,0:T(8,128)S(1)} copy-done((s32[12,12]{1,0:T(8,128)S(1)}, s32[12,12]{1,0:T(8,128)}, u32[]{:S(2)}) %copy-start.4) | copy-done | bytes 600
  6.1 0.0 copy-start.5
  6.1 0.7 %copy-done.5 = f32[3,384]{1,0:T(4,128)S(1)} copy-done((f32[3,384]{1,0:T(4,128)S(1)}, f32[3,384]{1,0:T(4,128)}, u32[]{:S(2)}) %copy-start.5) | copy-done | bytes 4632
  6.7 0.0 copy-start.6
  6.7 0.7 copy-done.6
  7.4 59.2 %shard_map.94 = (f32[2,768,128]{2,1,0:T(8,128)S(1)}, f32[6,128,128]{2,1,0:T(8,128)S(1)}, f32[3,128,128]{2,1,0:T(8,128)S(1)}) custom-call(f32[2,768,128]{2,1,0:T(8,128)S(1)} %copy-done.1, bf16[12,12,64,128]{3,2,1,0:T(8,128)(2,1)S(1)} %copy-done, s32[12,12]{1,0:T(8,128)S(1)} %copy-done.4, f32[3,384]{1,0:T(4,128)S(1)} %copy-done.5, s32[384]{0:T(512)S(1)} %copy-done.6, ...), custom_call_target="tpu_custom_call" | custom-call | tf_op jit(solution)/shard_map/pallas_call | solution.py:629
  66.6 0.9 %copy.15 = f32[2,768,128]{2,1,0:T(8,128)} copy(f32[2,768,128]{2,1,0:T(8,128)S(1)} %get-tuple-element.15) | data formatting | bytes 1572864
  67.5 0.7 %copy.16 = f32[6,1,128,128]{3,2,1,0:T(8,128)} copy(f32[6,1,128,128]{3,2,1,0:T(8,128)S(1)} %bitcast.9) | data formatting | bytes 786432
  68.2 0.7 copy.17
Async XLA Ops:
  0.6 1.7 %copy-start = (bf16[12,12,64,128]{3,2,1,0:T(8,128)(2,1)S(1)}, bf16[12,12,64,128]{3,2,1,0:T(8,128)(2,1)}, u32[]{:S(2)}) copy-start(bf16[12,12,64,128]{3,2,1,0:T(8,128)(2,1)} %ham_hbm.1) | copy-start | bytes 7077892
  2.3 1.1 %copy-start.1 = (f32[2,768,128]{2,1,0:T(8,128)S(1)}, f32[2,768,128]{2,1,0:T(8,128)}, u32[]{:S(2)}) copy-start(f32[2,768,128]{2,1,0:T(8,128)} %coef_hbm.1) | copy-start | bytes 2359300
  3.4 1.0 %copy-start.2 = (f32[6,1,128,128]{3,2,1,0:T(8,128)S(1)}, f32[6,1,128,128]{3,2,1,0:T(8,128)}, u32[]{:S(2)}) copy-start(f32[6,1,128,128]{3,2,1,0:T(8,128)} %param.12) | copy-start | bytes 1179652
  4.4 0.9 %copy-start.3 = (f32[3,1,128,128]{3,2,1,0:T(8,128)S(1)}, f32[3,1,128,128]{3,2,1,0:T(8,128)}, u32[]{:S(2)}) copy-start(f32[3,1,128,128]{3,2,1,0:T(8,128)} %param.13) | copy-start | bytes 589828
  5.4 0.7 %copy-start.4 = (s32[12,12]{1,0:T(8,128)S(1)}, s32[12,12]{1,0:T(8,128)}, u32[]{:S(2)}) copy-start(s32[12,12]{1,0:T(8,128)} %nbr.1) | copy-start | bytes 1732
  6.1 0.7 %copy-start.5 = (f32[3,384]{1,0:T(4,128)S(1)}, f32[3,384]{1,0:T(4,128)}, u32[]{:S(2)}) copy-start(f32[3,384]{1,0:T(4,128)} %pos.1) | copy-start | bytes 13828
  6.7 0.7 copy-start.6

commit v2 on v1

--- a/solution.py
+++ b/solution.py
@@ -33,12 +33,12 @@
 
 def kernel(
     groups, rows,
-    coef_hbm, ham_hbm, nbr, pos, site, field_hbm, pot_hbm,
-    coef_out, field_out, pot_out,
-    ham, placed, turned, phased, own, vp, halo, weights, inner,
+    coef_hbm, ham_hbm, nbr_hbm, pos_hbm, site_hbm, field_hbm, pot_hbm,
+    coef_res, field_res, pot_res,
+    coef_out, field_out, pot_out, nbr, pos, site, ham, placed, turned, phased, own, vp, halo, weights, inner,
     field, pot, e_send, e_recv, b_send, b_recv,
     at_send, at_recv, cur_send, cur_recv, posb, cos_tab, sin_tab, share,
-    in_sem, at_ss, at_rs, cur_ss, cur_rs, t_ss, t_rs, rim_ss, rim_rs,
+    in_sem, out_sem, at_ss, at_rs, cur_ss, cur_rs, t_ss, t_rs, rim_ss, rim_rs,
 ):
     atoms = nbr.shape[0]
     blocks = nbr.shape[1]
@@ -75,10 +75,11 @@
     has_up, has_down = r < rows - 1, r > 0
 
     loads = [
-        pltpu.make_async_copy(pot_hbm, pot, in_sem.at[0]),
-        pltpu.make_async_copy(coef_hbm, coef_out, in_sem.at[1]),
-        pltpu.make_async_copy(ham_hbm, ham, in_sem.at[2]),
-        pltpu.make_async_copy(field_hbm, field, in_sem.at[3]),
+        pltpu.make_async_copy(source, target, in_sem.at[i])
+        for i, (source, target) in enumerate((
+            (pot_hbm, pot), (coef_hbm, coef_out), (ham_hbm, ham), (field_hbm, field),
+            (site_hbm, site), (nbr_hbm, nbr), (pos_hbm, pos),
+        ))
     ]
     for load in loads:
         load.start()
@@ -118,6 +119,7 @@
     lax.fori_loop(0, sources, tell_sources, 0)
     lax.fori_loop(0, groups, tell_currents, 0)
 
+    loads[4].wait()
     first_here = lax.div(3 * s + 1, 2)
     second_ok = lax.rem(s, 2) == 0
     second_here = jnp.minimum(first_here + 1, atoms_all - 1)
@@ -127,8 +129,9 @@
     cell = iota((grid_y, grid_z), 0) * grid_z + iota((grid_y, grid_z), 1)
     at_one = cell == site_one
     at_two = cell == site_two
-    tile = (8, 128)
-    sub8, lane8 = iota(tile, 0), iota(tile, 1)
+    tile = (1, 128)
+    lane1 = iota(tile, 1)
+    comp_step = 32
 
     loads[0].wait()
     found = []
@@ -142,7 +145,7 @@
         for j in range(2):
             for c in range(3):
                 message = message + jnp.where(
-                    (sub8 == c) & (lane8 == lane_one + j), found[3 * j + c], 0.0
+                    lane1 == lane_one + j + comp_step * c, found[3 * j + c], 0.0
                 )
         at_send[k] = message
 
@@ -179,90 +182,8 @@
     for c in range(2):
         e_send[c] = field[1 + c].astype(BF16)
 
-    def ones(cond):
-        return jnp.where(cond, 1, 0)
-
-    expected = (
-        2 * groups
-        + groups * ones(other_ok)
-        - 2 * ones(q == r)
-        - ones(other_ok & (other == r))
-        + ones(has_next)
-        + ones(has_prev)
-    )
-    pl.semaphore_wait(barrier, expected)
-
-    def at_copy(k, slot, gg, rr):
-        return pltpu.make_async_remote_copy(
-            src_ref=at_send.at[k], dst_ref=at_recv.at[slot],
-            send_sem=at_ss.at[k, gg], recv_sem=at_rs.at[slot],
-            device_id=device(gg, rr), device_id_type=MESH,
-        )
-
-    slot_own = m + per_row // 2
-    slot_other = jnp.where(near, m + per_row + per_row // 2, m - per_row // 2)
-
-    def for_at_sends(action, keep):
-        for k, (target, slot, ok) in enumerate(
-            ((q, slot_own, None), (other, slot_other, other_ok))
-        ):
-            def one(gg, carry, k=k, target=target, slot=slot, ok=ok):
-                is_self = (gg == g) & (target == r)
-                go = jnp.logical_not(is_self)
-                if ok is not None:
-                    go = go & ok
-
-                @pl.when(go)
-                def _():
-                    action(at_copy(k, slot, gg, target))
-
-                if keep:
-                    @pl.when(is_self)
-                    def _():
-                        at_recv[slot] = at_send[k]
-
-                return carry
-
-            lax.fori_loop(0, groups, one, 0)
-
-    for_at_sends(lambda copy: copy.start(), True)
-
-    def t_copy(k, c, up):
-        side = 0 if up else 1
-        source = pl.ds(own_rows - half_rows, half_rows) if up else pl.ds(0, half_rows)
-        rr = next_r if up else prev_r
-        return pltpu.make_async_remote_copy(
-            src_ref=own.at[k, c, source, :], dst_ref=halo.at[k, c, side],
-            send_sem=t_ss.at[k, c, side], recv_sem=t_rs.at[k, c, side],
-            device_id=device(g, rr), device_id_type=MESH,
-        )
-
-    def send_term(k, c):
-        @pl.when(has_up)
-        def _():
-            t_copy(k, c, True).start()
-
-        @pl.when(has_down)
-        def _():
-            t_copy(k, c, False).start()
-
-    for c in range(CHUNKS):
-        send_term(0, c)
-
-    e_copy = pltpu.make_async_remote_copy(
-        src_ref=e_send, dst_ref=e_recv, send_sem=rim_ss.at[0], recv_sem=rim_rs.at[0],
-        device_id=device(prev_g, prev_r), device_id_type=MESH,
-    )
-    b_copy = pltpu.make_async_remote_copy(
-        src_ref=b_send, dst_ref=b_recv, send_sem=rim_ss.at[1], recv_sem=rim_rs.at[1],
-        device_id=device(next_g, next_r), device_id_type=MESH,
-    )
-
-    @pl.when(has_prev)
-    def _():
-        e_copy.start()
-
     loads[2].wait()
+    loads[5].wait()
     zero_block = jnp.zeros((orb, lanes), F32)
     chunk_rows = 16
 
@@ -294,11 +215,93 @@
         lax.fori_loop(0, orb // chunk_rows, piece, 0)
         return carry
 
-    lax.fori_loop(0, atoms, place, 0)
+    lax.fori_loop(0, atoms // 2, place, 0)
+
+    def ones(cond):
+        return jnp.where(cond, 1, 0)
+
+    expected = (
+        2 * groups
+        + groups * ones(other_ok)
+        - 2 * ones(q == r)
+        - ones(other_ok & (other == r))
+        + ones(has_next)
+        + ones(has_prev)
+    )
+    pl.semaphore_wait(barrier, expected)
+
+    def at_copy(k, slot, gg, rr):
+        return pltpu.make_async_remote_copy(
+            src_ref=at_send.at[k], dst_ref=at_recv.at[slot],
+            send_sem=at_ss.at[k, gg], recv_sem=at_rs.at[slot],
+            device_id=device(gg, rr), device_id_type=MESH,
+        )
+
+    slot_own = m + per_row // 2
+    slot_other = jnp.where(near, m + per_row + per_row // 2, m - per_row // 2)
+
+    def for_at_sends(action, keep):
+        for k, (target, slot, ok) in enumerate(
+            ((q, slot_own, None), (other, slot_other, other_ok))
+        ):
+            def one(gg, carry, k=k, target=target, slot=slot, ok=ok):
+                is_self = (gg == g) & (target == r)
+                go = jnp.logical_not(is_self)
+                if ok is not None:
+                    go = go & ok
+
+                @pl.when(go)
+                def _():
+                    action(at_copy(k, slot, gg, target))
+
+                if keep:
+                    @pl.when(is_self)
+                    def _():
+                        at_recv[slot] = at_send[k]
+
+                return carry
+
+            lax.fori_loop(0, groups, one, 0)
+
+    for_at_sends(lambda copy: copy.start(), True)
+
+    def t_copy(k, c, up):
+        side = 0 if up else 1
+        source = pl.ds(own_rows - half_rows, half_rows) if up else pl.ds(0, half_rows)
+        rr = next_r if up else prev_r
+        return pltpu.make_async_remote_copy(
+            src_ref=own.at[k, c, source, :], dst_ref=halo.at[k, c, side],
+            send_sem=t_ss.at[k, c, side], recv_sem=t_rs.at[k, c, side],
+            device_id=device(g, rr), device_id_type=MESH,
+        )
+
+    def send_term(k, c):
+        @pl.when(has_up)
+        def _():
+            t_copy(k, c, True).start()
+
+        @pl.when(has_down)
+        def _():
+            t_copy(k, c, False).start()
+
+    for c in range(CHUNKS):
+        send_term(0, c)
+
+    e_copy = pltpu.make_async_remote_copy(
+        src_ref=e_send, dst_ref=e_recv, send_sem=rim_ss.at[0], recv_sem=rim_rs.at[0],
+        device_id=device(prev_g, prev_r), device_id_type=MESH,
+    )
+    b_copy = pltpu.make_async_remote_copy(
+        src_ref=b_send, dst_ref=b_recv, send_sem=rim_ss.at[1], recv_sem=rim_rs.at[1],
+        device_id=device(next_g, next_r), device_id_type=MESH,
+    )
+
+    lax.fori_loop(atoms // 2, atoms, place, 0)
     for i in range(pairs):
         phased[i, 0:orb, (wide - 1) * lanes : wide * lanes] = zero_block.astype(BF16)
         phased[i, orb : 2 * orb, 0:lanes] = zero_block.astype(BF16)
 
+    loads[6].wait()
     posb[...] = jnp.zeros(posb.shape, F32)
     posb[0:3, 0:atoms_all] = pos[...]
     shift = lax.rem(2 * posb.shape[1] + reach - atoms * r, posb.shape[1])
@@ -335,7 +338,7 @@
 
     angle = jnp.zeros((16, 128), F32)
     for c in range(3):
-        row = at_near[c : c + 1, :]
+        row = pltpu.roll(at_near, 128 - comp_step * c, 1) if c else at_near
         angle = angle + 0.5 * (column(row, 1, reach) + row) * (pos_rows[c] - pos_cols[c])
     angle = coupling * angle
     cosine, sine = jnp.cos(angle), jnp.sin(angle)
@@ -445,34 +448,7 @@
 
     @pl.when(has_prev)
     def _():
-        e_copy.wait_send()
-
-    @pl.when(has_next)
-    def _():
-        e_copy.wait_recv()
-
-    comp = [field[c] for c in range(3)]
-    ahead = [jnp.where(has_next, e_recv[c].astype(F32), 0.0) for c in range(2)]
-
-    def ahead_y(v):
-        return shifted(v, 0, True) - v
-
-    def ahead_z(v):
-        return shifted(v, 1, True) - v
-
-    curl = (
-        ahead_y(comp[2]) - ahead_z(comp[1]),
-        ahead_z(comp[0]) - (ahead[1] - comp[2]),
-        (ahead[0] - comp[1]) - ahead_y(comp[0]),
-    )
-    for c in range(3):
-        field_out[3 + c] = field[3 + c] - wave_step * curl[c]
-    for c in range(2):
-        b_send[c] = field_out[4 + c].astype(BF16)
-
-    @pl.when(has_next)
-    def _():
-        b_copy.start()
+        e_copy.start()
 
     for c in range(CHUNKS):
         inner_products(1, c)
@@ -501,17 +477,14 @@
     share[...] = jnp.zeros(share.shape, F32)
     lax.fori_loop(0, pairs, shares, 0)
     scale = 1.0 / math.sqrt(2.0 * orb * groups * lanes)
-    for a in range(16):
-        if a >= atoms:
-            cur_send[a : a + 1, :] = jnp.zeros((1, 128), F32)
-            continue
+    line = jnp.zeros(tile, F32)
+    for a in range(atoms):
         each = jnp.sum(share[a], axis=1, keepdims=True)
-        line = jnp.zeros((1, 128), F32)
         for c in range(3):
             bond = column(pos_rows[c], 1, 2 * (a // 2)) - pos_cols[c][a : a + 1, :]
             value = scale * jnp.sum(each * bond, axis=0, keepdims=True)
-            line = line + jnp.where(iota((1, 128), 1) == c, value, 0.0)
-        cur_send[a : a + 1, :] = line
+            line = line + jnp.where(lane1 == 4 * a + c, value, 0.0)
+    cur_send[...] = line
 
     def cur_copy(i, slot, gg, rr):
         return pltpu.make_async_remote_copy(
@@ -543,6 +516,37 @@
     for c in range(CHUNKS):
         finish_term(1, c)
         send_term(2, c)
+    @pl.when(has_prev)
+    def _():
+        e_copy.wait_send()
+
+    @pl.when(has_next)
+    def _():
+        e_copy.wait_recv()
+
+    comp = [field[c] for c in range(3)]
+    ahead = [jnp.where(has_next, e_recv[c].astype(F32), 0.0) for c in range(2)]
+
+    def ahead_y(v):
+        return shifted(v, 0, True) - v
+
+    def ahead_z(v):
+        return shifted(v, 1, True) - v
+
+    curl = (
+        ahead_y(comp[2]) - ahead_z(comp[1]),
+        ahead_z(comp[0]) - (ahead[1] - comp[2]),
+        (ahead[0] - comp[1]) - ahead_y(comp[0]),
+    )
+    for c in range(3):
+        field_out[3 + c] = field[3 + c] - wave_step * curl[c]
+    for c in range(2):
+        b_send[c] = field_out[4 + c].astype(BF16)
+
+    @pl.when(has_next)
+    def _():
+        b_copy.start()
+
     for c in range(CHUNKS):
         inner_products(2, c)
     add_terms((1, 2))
@@ -569,8 +573,7 @@
     atom_one = first_here - atoms * q
 
     def picked(atom, c):
-        hit = jnp.where((sub16 == atom) & (lane16 == c), current, 0.0)
-        return jnp.sum(jnp.sum(hit, axis=0, keepdims=True), axis=1, keepdims=True)
+        return jnp.sum(jnp.where(lane1 == 4 * atom + c, current, 0.0), axis=1, keepdims=True)
 
     comp = [field_out[3 + c] for c in range(3)]
     behind = [jnp.where(has_prev, b_recv[c].astype(F32), 0.0) for c in range(2)]
@@ -594,9 +597,19 @@
         field_out[c] = electric
         pot_out[c] = pot[c] - wave_step * electric
 
+    stores = [
+        pltpu.make_async_copy(source, target, out_sem.at[i])
+        for i, (source, target) in enumerate(
+            ((field_out, field_res), (pot_out, pot_res), (coef_out, coef_res))
+        )
+    ]
+    stores[0].start()
+    stores[1].start()
+
     for c in range(CHUNKS):
         finish_term(2, c)
     add_terms((3,))
+    stores[2].start()
 
     for_at_sends(lambda copy: copy.wait_send(), False)
     for_cur_sends(lambda copy: copy.wait_send(), False)
@@ -609,6 +622,8 @@
             @pl.when(has_down)
             def _():
                 t_copy(k, c, False).wait_send()
+    for store in stores:
+        store.wait()
 
 
 def body(groups, rows, coefficients, hamiltonian, neighbours, positions, atom_site, rs_field, potential):
@@ -623,9 +638,7 @@
     field_in = rs_field.reshape((6,) + grid)
     pot_in = potential.reshape((3,) + grid)
     dma = pltpu.SemaphoreType.DMA
-    vmem = pl.BlockSpec(memory_space=pltpu.VMEM)
-    smem = pl.BlockSpec(memory_space=pltpu.SMEM)
-    hbm = pl.BlockSpec(memory_space=pl.ANY)
+    hbm = pl.BlockSpec(memory_space=pltpu.HBM)
     coef, field, pot = pl.pallas_call(
         functools.partial(kernel, groups, rows),
         out_shape=(
@@ -633,9 +646,15 @@
             jax.ShapeDtypeStruct(field_in.shape, F32),
             jax.ShapeDtypeStruct(pot_in.shape, F32),
         ),
-        in_specs=[hbm, hbm, smem, vmem, smem, hbm, hbm],
-        out_specs=(vmem, vmem, vmem),
+        in_specs=[hbm] * 7,
+        out_specs=(hbm, hbm, hbm),
         scratch_shapes=[
+            pltpu.VMEM(coefficients.shape, F32),
+            pltpu.VMEM(field_in.shape, F32),
+            pltpu.VMEM(pot_in.shape, F32),
+            pltpu.SMEM(neighbours.shape, jnp.int32),
+            pltpu.VMEM(positions.shape, F32),
+            pltpu.SMEM(atom_site.shape, jnp.int32),
             pltpu.VMEM(hamiltonian.shape, BF16),
             pltpu.VMEM((pairs, 2 * orb, wide * lanes), F32),
             pltpu.VMEM((pairs, 2 * orb, wide * lanes), F32),
@@ -651,15 +670,16 @@
             pltpu.VMEM((2,) + grid, BF16),
             pltpu.VMEM((2,) + grid, BF16),
             pltpu.VMEM((2,) + grid, BF16),
-            pltpu.VMEM((2, 8, 128), F32),
-            pltpu.VMEM((2 * per_row, 8, 128), F32),
-            pltpu.VMEM((16, 128), F32),
-            pltpu.VMEM((groups, 16, 128), F32),
+            pltpu.VMEM((2, 1, 128), F32),
+            pltpu.VMEM((2 * per_row, 1, 128), F32),
+            pltpu.VMEM((1, 128), F32),
+            pltpu.VMEM((groups, 1, 128), F32),
             pltpu.VMEM((8, 512), F32),
             pltpu.VMEM((16, 128), F32),
             pltpu.VMEM((16, 128), F32),
             pltpu.VMEM((atoms, 16, 128), F32),
-            dma((4,)),
+            dma((7,)),
+            dma((3,)),
             dma((2, groups)),
             dma((2 * per_row,)),
             dma((per_row,)),
@@ -670,7 +690,7 @@
             dma((2,)),
         ],
         compiler_params=pltpu.CompilerParams(
-            collective_id=0, has_side_effects=True, vmem_limit_bytes=48 * 2**20
+            collective_id=0, has_side_effects=True, vmem_limit_bytes=60 * 2**20
         ),
     )(coefficients, hamiltonian, neighbours, positions, atom_site, field_in, pot_in)
     return coef, field.reshape(rs_field.shape), pot.reshape(potential.shape)

time: 69.2 us -> 58.3 us (0.84)
  the two profiles are of different devices: /device:TPU:94 before, /device:TPU:41 now
where the time goes in v2:
time: 58.3 us; the launch traced here: 58.1 us
  Pallas kernels  52.9 us (91%)
  local copies, waits for them, and re-layouts  4.55 us (8%)
  between operations  0.65 us (1%)
    pallas_call x1, Pallas kernels, body(): pl.pallas_call(functools.partial(kernel, groups, rows), out_shape=(jax.Sh...  52.9 us
    unnamed x5, local copies, waits for them, and re-layouts  4.55 us

profile of v2, /device:TPU:41, one launch (start us, length us, event | category | flops | bytes accessed | tf_op | source)
XLA Modules:
  0.0 58.1 jit_solution(8126605706250573764)
XLA Ops:
  0.6 52.9 %shard_map.94 = (f32[2,768,128]{2,1,0:T(8,128)}, f32[6,128,128]{2,1,0:T(8,128)}, f32[3,128,128]{2,1,0:T(8,128)}) custom-call(f32[2,768,128]{2,1,0:T(8,128)} %coef_hbm.1, bf16[12,12,64,128]{3,2,1,0:T(8,128)(2,1)} %ham_hbm.1, s32[12,12]{1,0:T(8,128)} %nbr_hbm.1, f32[3,384]{1,0:T(4,128)} %pos_hbm.1, s32[384]{0:T(512)} %site_hbm.1, f32[6,128,128]{2,1,0:T(8,128)} %bitcast.8, ...), custom_call_target="tpu_custom_call" | custom-call | tf_op jit(solution)/shard_map/pallas_call | solution.py:642
  53.6 0.0 copy-start
  53.6 2.1 %copy.15 = f32[2,768,128]{2,1,0:T(8,128)} copy(f32[2,768,128]{2,1,0:T(8,128)} %get-tuple-element.15) | data formatting | bytes 1572864
  55.7 1.8 %copy.16 = f32[6,1,128,128]{3,2,1,0:T(8,128)} copy(f32[6,1,128,128]{3,2,1,0:T(8,128)} %bitcast.9) | data formatting | bytes 786432
  57.4 0.0 copy-done
  57.4 0.7 %copy.17 = f32[3,1,128,128]{3,2,1,0:T(8,128)} copy(f32[3,1,128,128]{3,2,1,0:T(8,128)S(1)} %bitcast.11) | data formatting | bytes 393216
Async XLA Ops:
  53.6 3.9 %copy-start = (f32[3,128,128]{2,1,0:T(8,128)S(1)}, f32[3,128,128]{2,1,0:T(8,128)}, u32[]{:S(2)}) copy-start(f32[3,128,128]{2,1,0:T(8,128)} %get-tuple-element.8) | copy-start | bytes 589828

commit v3 on v2

--- a/solution.py
+++ b/solution.py
@@ -284,8 +284,7 @@
         def _():
             t_copy(k, c, False).start()
 
-    for c in range(CHUNKS):
-        send_term(0, c)
+    send_term(0, 0)
 
     e_copy = pltpu.make_async_remote_copy(
         src_ref=e_send, dst_ref=e_recv, send_sem=rim_ss.at[0], recv_sem=rim_rs.at[0],
@@ -297,6 +296,13 @@
     )
 
     lax.fori_loop(atoms // 2, atoms, place, 0)
+    for c in range(1, CHUNKS):
+        send_term(0, c)
+
+    @pl.when(has_prev)
+    def _():
+        e_copy.start()
+
     for i in range(pairs):
         phased[i, 0:orb, (wide - 1) * lanes : wide * lanes] = zero_block.astype(BF16)
         phased[i, orb : 2 * orb, 0:lanes] = zero_block.astype(BF16)
@@ -421,6 +427,13 @@
                 )
                 rotated = product.astype(BF16)
                 value = (turn(product) * out_signs).astype(BF16)
+                if k + 1 == TERMS and c + 1 == CHUNKS:
+                    first = own[k + 1, 0, at, :].astype(F32)
+                    second = value.astype(F32)
+                    low = iota((1, lanes), 1) < orb
+                    coef_out[0, at, :] = coef_out[0, at, :] + jnp.where(low, first, turn(second))
+                    coef_out[1, at, :] = coef_out[1, at, :] + jnp.where(low, turn(first), second)
+                    continue
                 own[k + 1, c, at, :] = value
                 if k + 1 < TERMS:
                     for j in range(2):
@@ -445,12 +458,6 @@
     for c in range(CHUNKS):
         finish_term(0, c)
         send_term(1, c)
-
-    @pl.when(has_prev)
-    def _():
-        e_copy.start()
-
-    for c in range(CHUNKS):
         inner_products(1, c)
 
     def shares(i, carry):
@@ -513,9 +520,6 @@
 
     for_cur_sends(lambda copy: copy.start(), True)
 
-    for c in range(CHUNKS):
-        finish_term(1, c)
-        send_term(2, c)
     @pl.when(has_prev)
     def _():
         e_copy.wait_send()
@@ -548,6 +552,8 @@
         b_copy.start()
 
     for c in range(CHUNKS):
+        finish_term(1, c)
+        send_term(2, c)
         inner_products(2, c)
     add_terms((1, 2))
 
@@ -608,7 +614,6 @@
 
     for c in range(CHUNKS):
         finish_term(2, c)
-    add_terms((3,))
     stores[2].start()
 
     for_at_sends(lambda copy: copy.wait_send(), False)
@@ -622,6 +627,28 @@
             @pl.when(has_down)
             def _():
                 t_copy(k, c, False).wait_send()
+    for store in stores:
+        store.wait()
+
+
+def hand_on(coef, field, pot, coef_out, field_out, pot_out, coef_buf, field_buf, pot_buf, in_sem, out_sem):
+    half = coef.shape[1] // 2
+    pieces = [(pot, pot_buf, pot_out)]
+    for i in range(2):
+        pieces.append([ref.at[pl.ds(3 * i, 3)] for ref in (field, field_buf, field_out)])
+        for part in range(2):
+            at = pl.ds(part * half, half)
+            pieces.append([ref.at[i, at] for ref in (coef, coef_buf, coef_out)])
+    loads, stores = [], []
+    for i, piece in enumerate(pieces):
+        source, held, target = piece
+        loads.append(pltpu.make_async_copy(source, held, in_sem.at[i]))
+        stores.append(pltpu.make_async_copy(held, target, out_sem.at[i]))
+    for load in loads:
+        load.start()
+    for load, store in zip(loads, stores):
+        load.wait()
+        store.start()
     for store in stores:
         store.wait()
 
@@ -693,6 +720,24 @@
             collective_id=0, has_side_effects=True, vmem_limit_bytes=60 * 2**20
         ),
     )(coefficients, hamiltonian, neighbours, positions, atom_site, field_in, pot_in)
+    coef, field, pot = pl.pallas_call(
+        hand_on,
+        out_shape=(
+            jax.ShapeDtypeStruct(coefficients.shape, F32),
+            jax.ShapeDtypeStruct(field_in.shape, F32),
+            jax.ShapeDtypeStruct(pot_in.shape, F32),
+        ),
+        in_specs=[hbm, hbm, hbm],
+        out_specs=(hbm, hbm, hbm),
+        scratch_shapes=[
+            pltpu.VMEM(coefficients.shape, F32),
+            pltpu.VMEM(field_in.shape, F32),
+            pltpu.VMEM(pot_in.shape, F32),
+            dma((8,)),
+            dma((8,)),
+        ],
+        compiler_params=pltpu.CompilerParams(vmem_limit_bytes=60 * 2**20),
+    )(coef, field, pot)
     return coef, field.reshape(rs_field.shape), pot.reshape(potential.shape)
 
 

time: 58.3 us -> 54.2 us (0.930)
  the two profiles are of different devices: /device:TPU:41 before, /device:TPU:49 now
where the time goes in v3:
time: 54.2 us; the launch traced here: 54.1 us
  Pallas kernels  53.5 us (99%)
  between operations  0.64 us (1%)
    pallas_call x1, Pallas kernels, body(): pl.pallas_call(functools.partial(kernel, groups, rows), out_shape=(jax.Sh...  51.2 us
    pallas_call x1, Pallas kernels, body(): pl.pallas_call(hand_on, out_shape=(jax.ShapeDtypeStruct(coefficients.shap...  2.23 us

profile of v3, /device:TPU:49, one launch (start us, length us, event | category | flops | bytes accessed | tf_op | source)
XLA Modules:
  0.0 54.1 jit_solution(3809237737720867647)
XLA Ops:
  0.6 51.2 %shard_map.94 = (f32[2,768,128]{2,1,0:T(8,128)}, f32[6,128,128]{2,1,0:T(8,128)}, f32[3,128,128]{2,1,0:T(8,128)}) custom-call(f32[2,768,128]{2,1,0:T(8,128)} %coef_hbm.1, bf16[12,12,64,128]{3,2,1,0:T(8,128)(2,1)} %ham_hbm.1, s32[12,12]{1,0:T(8,128)} %nbr_hbm.1, f32[3,384]{1,0:T(4,128)} %pos_hbm.1, s32[384]{0:T(512)} %site_hbm.1, f32[6,128,128]{2,1,0:T(8,128)} %bitcast.8, ...), custom_call_target="tpu_custom_call" | custom-call | tf_op jit(solution)/shard_map/pallas_call | solution.py:669
  51.9 2.2 %shard_map.95 = (f32[2,768,128]{2,1,0:T(8,128)}, f32[6,128,128]{2,1,0:T(8,128)}, f32[3,128,128]{2,1,0:T(8,128)}) custom-call(f32[2,768,128]{2,1,0:T(8,128)} %get-tuple-element.9.coef, f32[6,128,128]{2,1,0:T(8,128)} %get-tuple-element.10.field, f32[3,128,128]{2,1,0:T(8,128)} %get-tuple-element.11.pot), custom_call_target="tpu_custom_call" | custom-call | tf_op jit(solution)/shard_map/pallas_call | solution.py:723

commit v4 on v3

--- a/solution.py
+++ b/solution.py
@@ -117,7 +117,6 @@
         tell(prev_g, prev_r)
 
     lax.fori_loop(0, sources, tell_sources, 0)
-    lax.fori_loop(0, groups, tell_currents, 0)
 
     loads[4].wait()
     first_here = lax.div(3 * s + 1, 2)
@@ -185,7 +184,7 @@
     loads[2].wait()
     loads[5].wait()
     zero_block = jnp.zeros((orb, lanes), F32)
-    chunk_rows = 16
+    chunk_rows = 32
 
     def place(a, carry):
         i = lax.div(a, 2)
@@ -215,15 +214,13 @@
         lax.fori_loop(0, orb // chunk_rows, piece, 0)
         return carry
 
-    lax.fori_loop(0, atoms // 2, place, 0)
-
     def ones(cond):
         return jnp.where(cond, 1, 0)
 
     expected = (
-        2 * groups
+        groups
         + groups * ones(other_ok)
-        - 2 * ones(q == r)
+        - ones(q == r)
         - ones(other_ok & (other == r))
         + ones(has_next)
         + ones(has_prev)
@@ -295,10 +292,11 @@
         device_id=device(next_g, next_r), device_id_type=MESH,
     )
 
-    lax.fori_loop(atoms // 2, atoms, place, 0)
+    lax.fori_loop(0, 6, place, 0)
     for c in range(1, CHUNKS):
         send_term(0, c)
 
+    lax.fori_loop(6, atoms, place, 0)
     @pl.when(has_prev)
     def _():
         e_copy.start()

time: 54.2 us -> 52.2 us (0.963)
  the two profiles are of different devices: /device:TPU:49 before, /device:TPU:17 now
where the time goes in v4:
time: 52.2 us; the launch traced here: 52 us
  Pallas kernels  51.3 us (98%)
  between operations  0.64 us (1%)
    pallas_call x1, Pallas kernels, body(): pl.pallas_call(functools.partial(kernel, groups, rows), out_shape=(jax.Sh...  49.1 us
    pallas_call x1, Pallas kernels, body(): pl.pallas_call(hand_on, out_shape=(jax.ShapeDtypeStruct(coefficients.shap...  2.23 us

profile of v4, /device:TPU:17, one launch (start us, length us, event | category | flops | bytes accessed | tf_op | source)
XLA Modules:
  0.0 52.0 jit_solution(3514436467735135903)
XLA Ops:
  0.6 49.1 %shard_map.94 = (f32[2,768,128]{2,1,0:T(8,128)}, f32[6,128,128]{2,1,0:T(8,128)}, f32[3,128,128]{2,1,0:T(8,128)}) custom-call(f32[2,768,128]{2,1,0:T(8,128)} %coef_hbm.1, bf16[12,12,64,128]{3,2,1,0:T(8,128)(2,1)} %ham_hbm.1, s32[12,12]{1,0:T(8,128)} %nbr_hbm.1, f32[3,384]{1,0:T(4,128)} %pos_hbm.1, s32[384]{0:T(512)} %site_hbm.1, f32[6,128,128]{2,1,0:T(8,128)} %bitcast.8, ...), custom_call_target="tpu_custom_call" | custom-call | tf_op jit(solution)/shard_map/pallas_call | solution.py:667
  49.7 2.2 %shard_map.95 = (f32[2,768,128]{2,1,0:T(8,128)}, f32[6,128,128]{2,1,0:T(8,128)}, f32[3,128,128]{2,1,0:T(8,128)}) custom-call(f32[2,768,128]{2,1,0:T(8,128)} %get-tuple-element.9.coef, f32[6,128,128]{2,1,0:T(8,128)} %get-tuple-element.10.field, f32[3,128,128]{2,1,0:T(8,128)} %get-tuple-element.11.pot), custom_call_target="tpu_custom_call" | custom-call | tf_op jit(solution)/shard_map/pallas_call | solution.py:721

commit v5 on v4

--- a/solution.py
+++ b/solution.py
@@ -272,12 +272,21 @@
             device_id=device(g, rr), device_id_type=MESH,
         )
 
+    def send_side(k, c, up):
+        @pl.when(has_up if up else has_down)
+        def _():
+            t_copy(k, c, up).start()
+
     def send_term(k, c):
-        @pl.when(has_up)
+        down_first = lax.rem(r, 4) == 0
+
+        @pl.when(down_first & has_down)
         def _():
-            t_copy(k, c, True).start()
-
-        @pl.when(has_down)
+            t_copy(k, c, False).start()
+
+        send_side(k, c, True)
+
+        @pl.when(jnp.logical_not(down_first) & has_down)
         def _():
             t_copy(k, c, False).start()
 
@@ -407,7 +416,7 @@
     def finish_term(k, c):
         par = k % 2
         factor = elec_step / (k + 1)
-        for up_side in (False, True):
+        for up_side in (True, False):
             take_halo(k, c, up_side)
             for i in range(pairs // 2):
                 if up_side:
@@ -439,6 +448,8 @@
                         part = slice(j * orb, (j + 1) * orb)
                         weights[1 - par, c, base : base + orb, :] = value[part]
                         weights[1 - par, c, base + orb : base + lanes, :] = rotated[part]
+            if k + 1 < TERMS:
+                send_side(k + 1, c, up_side)
 
     def add_terms(which):
         def one(a, carry):
@@ -453,9 +464,8 @@
 
     for c in range(CHUNKS):
         inner_products(0, c)
+        finish_term(0, c)
     for c in range(CHUNKS):
-        finish_term(0, c)
-        send_term(1, c)
         inner_products(1, c)
 
     def shares(i, carry):
@@ -551,7 +561,6 @@
 
     for c in range(CHUNKS):
         finish_term(1, c)
-        send_term(2, c)
         inner_products(2, c)
     add_terms((1, 2))
 

time: 52.2 us -> 51.6 us (0.989)
  no operation moved by 1% of the time
where the time goes in v5:
time: 51.6 us; the launch traced here: 51.5 us
  Pallas kernels  50.9 us (99%)
  between operations  0.64 us (1%)
    pallas_call x1, Pallas kernels, body(): pl.pallas_call(functools.partial(kernel, groups, rows), out_shape=(jax.Sh...  48.6 us
    pallas_call x1, Pallas kernels, body(): pl.pallas_call(hand_on, out_shape=(jax.ShapeDtypeStruct(coefficients.shap...  2.23 us

profile of v5, /device:TPU:17, one launch (start us, length us, event | category | flops | bytes accessed | tf_op | source)
XLA Modules:
  0.0 51.5 jit_solution(17927704331216204419)
XLA Ops:
  0.6 48.6 %shard_map.94 = (f32[2,768,128]{2,1,0:T(8,128)}, f32[6,128,128]{2,1,0:T(8,128)}, f32[3,128,128]{2,1,0:T(8,128)}) custom-call(f32[2,768,128]{2,1,0:T(8,128)} %coef_hbm.1, bf16[12,12,64,128]{3,2,1,0:T(8,128)(2,1)} %ham_hbm.1, s32[12,12]{1,0:T(8,128)} %nbr_hbm.1, f32[3,384]{1,0:T(4,128)} %pos_hbm.1, s32[384]{0:T(512)} %site_hbm.1, f32[6,128,128]{2,1,0:T(8,128)} %bitcast.8, ...), custom_call_target="tpu_custom_call" | custom-call | tf_op jit(solution)/shard_map/pallas_call | solution.py:676
  49.3 2.2 %shard_map.95 = (f32[2,768,128]{2,1,0:T(8,128)}, f32[6,128,128]{2,1,0:T(8,128)}, f32[3,128,128]{2,1,0:T(8,128)}) custom-call(f32[2,768,128]{2,1,0:T(8,128)} %get-tuple-element.9.coef, f32[6,128,128]{2,1,0:T(8,128)} %get-tuple-element.10.field, f32[3,128,128]{2,1,0:T(8,128)} %get-tuple-element.11.pot), custom_call_target="tpu_custom_call" | custom-call | tf_op jit(solution)/shard_map/pallas_call | solution.py:730

commit v6 on v5

--- a/solution.py
+++ b/solution.py
@@ -116,7 +116,7 @@
     def _():
         tell(prev_g, prev_r)
 
-    lax.fori_loop(0, sources, tell_sources, 0)
+    lax.fori_loop(0, sources, tell_sources, 0, unroll=4)
 
     loads[4].wait()
     first_here = lax.div(3 * s + 1, 2)
@@ -258,7 +258,7 @@
 
                 return carry
 
-            lax.fori_loop(0, groups, one, 0)
+            lax.fori_loop(0, groups, one, 0, unroll=4)
 
     for_at_sends(lambda copy: copy.start(), True)
 

time: 51.6 us -> 51.6 us (level)
  no operation moved by 1% of the time
where the time goes in v6:
time: 51.6 us; the launch traced here: 51.5 us
  Pallas kernels  50.8 us (98%)
  between operations  0.64 us (1%)
    pallas_call x1, Pallas kernels, body(): pl.pallas_call(functools.partial(kernel, groups, rows), out_shape=(jax.Sh...  48.6 us
    pallas_call x1, Pallas kernels, body(): pl.pallas_call(hand_on, out_shape=(jax.ShapeDtypeStruct(coefficients.shap...  2.23 us

profile of v6, /device:TPU:17, one launch (start us, length us, event | category | flops | bytes accessed | tf_op | source)
XLA Modules:
  0.0 51.5 jit_solution(16294813558319621084)
XLA Ops:
  0.6 48.6 %shard_map.94 = (f32[2,768,128]{2,1,0:T(8,128)}, f32[6,128,128]{2,1,0:T(8,128)}, f32[3,128,128]{2,1,0:T(8,128)}) custom-call(f32[2,768,128]{2,1,0:T(8,128)} %coef_hbm.1, bf16[12,12,64,128]{3,2,1,0:T(8,128)(2,1)} %ham_hbm.1, s32[12,12]{1,0:T(8,128)} %nbr_hbm.1, f32[3,384]{1,0:T(4,128)} %pos_hbm.1, s32[384]{0:T(512)} %site_hbm.1, f32[6,128,128]{2,1,0:T(8,128)} %bitcast.8, ...), custom_call_target="tpu_custom_call" | custom-call | tf_op jit(solution)/shard_map/pallas_call | solution.py:676
  49.2 2.2 %shard_map.95 = (f32[2,768,128]{2,1,0:T(8,128)}, f32[6,128,128]{2,1,0:T(8,128)}, f32[3,128,128]{2,1,0:T(8,128)}) custom-call(f32[2,768,128]{2,1,0:T(8,128)} %get-tuple-element.9.coef, f32[6,128,128]{2,1,0:T(8,128)} %get-tuple-element.10.field, f32[3,128,128]{2,1,0:T(8,128)} %get-tuple-element.11.pot), custom_call_target="tpu_custom_call" | custom-call | tf_op jit(solution)/shard_map/pallas_call | solution.py:730
